TPU v7x, 32 devices: a whole 2x2x4 slice. The times are simulated.
32 devices in a mesh: seq: 16 (over z, y, x), doc: 2 (over core).
Axes of the slice: x: 2, y: 2, z: 4, core: 2. Of those that a mesh axis runs over, the one named last changes fastest.
Arguments:
- conv_input: bfloat16 [4096, 4352], P(('doc', 'seq')), parts along dimension 0, may hold values from -6 to 6
- gate_input: bfloat16 [4096, 4096], P(('doc', 'seq')), parts along dimension 0, may hold values from -6 to 6
- step_input: bfloat16 [4096, 64], P(('doc', 'seq')), parts along dimension 0, may hold values from -1.1 to 2.9
- conv_weight: float32 [4, 4352], replicated, may hold values from -3 to 3
- convolution_bias: float32 [4352], replicated, may hold values from -0.5 to 0.5
- step_bias: float32 [64], replicated, may hold values from -12 to -2, as said below
- decay_log: float32 [64], replicated, may hold values from -3.3 to -1, as said below
- skip_gain: float32 [64], replicated, may hold values from 0.5 to 2
- norm_gain: float32 [4096], replicated, may hold values from 0.5 to 1.5
Outputs:
- normed: bfloat16 [4096, 4096], P(('doc', 'seq')), parts along dimension 0
There are 2 independent parts, one for each index of `doc`. A program takes and returns all parts, laid end to end along the dimension named above; an argument that names none is the same for every part. Nothing has to cross between parts.
Inputs may be any that keep to these rules, and one draw needn't show every extreme that they name: `decay_log`: one value a head. `step_bias`: one value a head.
All inputs are finite; a program needn't handle non-finite values.
Results may differ from a plain program's by a relative error of at most 0.0051.
Values may be sent and summed in bfloat16 or wider, within the bound.
A program may use at most 64 MiB of HBM per device.

v0:
```python
import jax
import jax.numpy as jnp
from jax import lax
from jax.sharding import PartitionSpec as P

HEADDIM = 64
STATE = 128
HEADS = 64
STRETCH = 256


def shifted(value, axis, steps):
    count = lax.axis_size(axis)
    initial, last = (max(0, -steps), min(count, count - steps))
    return lax.ppermute(value, axis, [(source, source + steps) for source in range(initial, last)])


def gated_norm(mixed_out, gate_input, norm_gain):
    gated = mixed_out.astype(jnp.float32) * jax.nn.silu(gate_input.astype(jnp.float32))
    spread = jnp.mean(gated * gated, axis=-1, keepdims=True)
    return (gated * lax.rsqrt(spread + 1e-05) * norm_gain[None, :]).astype(jnp.bfloat16)


def convolve(conv_input, conv_weight, convolution_bias):
    tap_count = conv_weight.shape[0]
    row_count = conv_input.shape[0]
    earlier = shifted(conv_input[row_count - (tap_count - 1) :], "seq", 1)
    padded = jnp.concatenate([earlier, conv_input], axis=0).astype(jnp.float32)
    mixed = convolution_bias[None, :]
    for offset in range(tap_count):
        mixed = mixed + conv_weight[offset][None, :] * padded[offset : offset + row_count]
    return jax.nn.silu(mixed).astype(jnp.bfloat16)


def dual_form(values, step_size, decay_rate, b_rows, c_rows, block_len):
    highest = lax.Precision.HIGHEST
    row_count, head_count, head_width = values.shape
    state_width = b_rows.shape[1]
    blocks = row_count // block_len
    block_values = values.reshape(blocks, block_len, head_count, head_width)
    block_step_sizes = step_size.reshape(blocks, block_len, head_count)
    block_b = b_rows.reshape(blocks, block_len, state_width)
    block_c = c_rows.reshape(blocks, block_len, state_width)
    within = jnp.cumsum(block_step_sizes * decay_rate[None, None, :], axis=1)
    ends = within[:, -1, :]
    totals = jnp.cumsum(ends, axis=0)
    before = totals - ends
    lower = jnp.arange(block_len)[:, None] >= jnp.arange(block_len)[None, :]
    turned = jnp.transpose(within, (0, 2, 1))
    diffs = jnp.where(lower[None, None], turned[:, :, :, None] - turned[:, :, None, :], -jnp.inf)
    scores = jnp.einsum("ctn,csn->cts", block_c, block_b, precision=highest)
    mixing = (
        jnp.exp(diffs) * scores[:, None] * jnp.transpose(block_step_sizes, (0, 2, 1))[:, :, None, :]
    )
    inside = jnp.einsum("chts,cshp->cthp", mixing, block_values, precision=highest)
    tail = jnp.exp(ends[:, None, :] - within) * block_step_sizes
    weighted = tail[:, :, :, None] * block_values
    states = jnp.einsum("cshp,csn->chpn", weighted, block_b, precision=highest)
    order = jnp.arange(blocks)
    earlier_mask = order[:, None] > order[None, :]
    gap = jnp.where(earlier_mask[None], before.T[:, :, None] - totals.T[:, None, :], -jnp.inf)
    entering = jnp.einsum("hcd,dhpn->chpn", jnp.exp(gap), states, precision=highest)
    outside = jnp.exp(within)[:, :, :, None] * jnp.einsum(
        "ctn,chpn->cthp", block_c, entering, precision=highest
    )
    result = (inside + outside).reshape(row_count, head_count, head_width)
    last = totals[-1]
    final = jnp.einsum("dh,dhpn->hpn", jnp.exp(last[None, :] - totals), states, precision=highest)
    decay_sum = (before[:, None, :] + within).reshape(row_count, head_count)
    return (result, final, decay_sum, last)


def shards(
    conv_input,
    gate_input,
    step_input,
    conv_weight,
    convolution_bias,
    step_bias,
    decay_log,
    skip_gain,
    norm_gain,
):
    inner_width = HEADS * HEADDIM
    decay_rate = -jnp.exp(decay_log)
    activated = convolve(conv_input, conv_weight, convolution_bias)
    head_values, head_steps = (
        lax.all_to_all(activated[:, :inner_width], "seq", split_axis=1, concat_axis=0, tiled=True),
        lax.all_to_all(step_input, "seq", split_axis=1, concat_axis=0, tiled=True),
    )
    shared = lax.all_gather(activated[:, inner_width:], "seq", axis=0, tiled=True)
    full_rows = shared.shape[0]
    own_heads = head_steps.shape[1]
    first_head = lax.axis_index("seq") * own_heads
    own_bias = lax.dynamic_slice_in_dim(step_bias, first_head, own_heads)
    own_rate = lax.dynamic_slice_in_dim(decay_rate, first_head, own_heads)
    own_skip = lax.dynamic_slice_in_dim(skip_gain, first_head, own_heads)
    values = head_values.astype(jnp.float32).reshape(full_rows, own_heads, HEADDIM)
    shared_rows = shared.astype(jnp.float32)
    step_size = jax.nn.softplus(head_steps.astype(jnp.float32) + own_bias[None, :])
    result, final, decay_sum, last = dual_form(
        values,
        step_size,
        own_rate,
        shared_rows[:, :STATE],
        shared_rows[:, STATE:],
        min(STRETCH, full_rows),
    )
    result = result + own_skip[None, :, None] * values
    head_output = result.astype(jnp.bfloat16).reshape(full_rows, own_heads * HEADDIM)
    mixed_out = lax.all_to_all(head_output, "seq", split_axis=0, concat_axis=1, tiled=True)
    return gated_norm(mixed_out, gate_input, norm_gain)


def solution(mesh):
    in_specs = (
        P(("doc", "seq"), None),
        P(("doc", "seq"), None),
        P(("doc", "seq"), None),
        P(),
        P(),
        P(),
        P(),
        P(),
        P(),
    )
    out_specs = P(("doc", "seq"), None)
    return jax.shard_map(shards, mesh=mesh, in_specs=in_specs, out_specs=out_specs, check_vma=False)
```

profile of v0, /device:TPU:24, one launch (start us, length us, event | category | flops | bytes accessed | tf_op | source)
XLA Modules:
  0.0 144.4 jit_solution(9924083408817625690)
XLA Ops:
  6.5 7.1 %all-to-all-start.1 = ((bf16[128,16,4]{0,2,1:T(4,128)(2,1)}), bf16[128,16,4]{0,2,1:T(4,128)(2,1)S(1)}, u32[]{:S(2)}, u32[]{:S(2)}) async-start(bf16[128,16,4]{0,2,1:T(4,128)(2,1)} %bitcast.77), calls=%async_computation.1 | async-start | bytes 32768 | tf_op jit(solution)/shard_map/all_to_all | solution.py:89
  13.7 0.0 all-gather.2.cloned.1.call-start
  13.7 0.9 slice.49
  14.6 3.4 %collective-permute-start = (bf16[3,4352]{1,0:T(4,128)(2,1)S(1)}, bf16[3,4352]{1,0:T(4,128)(2,1)S(1)}, u32[]{:S(2)}, u32[]{:S(2)}) collective-permute-start(bf16[3,4352]{1,0:T(4,128)(2,1)S(1)} %slice.49), channel_id=1, source_target_pairs={{0,2},{2,4},{4,6},{6,8},{8,10},{10,12},{12,14},{14,16},{16,18},{18... | collective-permute-start | bytes 78344 | tf_op jit(solution)/shard_map/ppermute | solution.py:15
  18.0 1.2 slice_reduce_fusion.4
  19.2 1.7 %copy.46 = bf16[128,4352]{0,1:T(8,128)(2,1)S(1)} copy(bf16[128,4352]{1,0:T(8,128)(2,1)} %param.9) | data formatting | bytes 2228224 | tf_op args[0]
  20.9 0.1 dynamic_slice.9
  21.0 1.2 collective-permute-done
  22.3 0.5 copy.45
  22.8 0.8 maximum_convert_fusion
  23.6 5.5 %multiply_convert_fusion = bf16[128,4352]{0,1:T(8,128)(2,1)S(1)} fusion(f32[131,4352]{0,1:T(8,128)S(1)} %maximum_convert_fusion, f32[4352]{0:T(1024)S(1)} %get-tuple-element.7, f32[4352]{0:T(1024)S(1)} %get-tuple-element.8, f32[4352]{0:T(1024)S(1)} %get-tuple-element.6, f32[4352]{0:T(1024)S(1)} %get-tuple-element.5, f32[4352]{0:T(1024)S(1)} %copy-done.1), kind=kLoop, calls=%fused_computation.23 | loop fusion | flops 7241728 | bytes 10114048 | tf_op jit(solution)/shard_map/convert_element_type | solution.py:32
  29.2 1.0 slice.68
  30.2 0.6 slice.71
  30.8 0.0 all-gather.2.cloned.1.call-update
  30.9 5.1 %all-to-all-start = ((bf16[128,16,256]{0,2,1:T(8,128)(2,1)}), bf16[128,16,256]{0,2,1:T(8,128)(2,1)S(1)}, u32[]{:S(2)}, u32[]{:S(2)}) async-start(bf16[128,16,256]{0,2,1:T(8,128)(2,1)} %bitcast), calls=%async_computation | async-start | bytes 2097152 | tf_op jit(solution)/shard_map/all_to_all | solution.py:88
  36.0 0.1 dynamic_slice.10
  36.1 0.1 dynamic_slice.11
  36.2 0.1 mul.155
  36.2 0.1 mul.156
  36.4 0.1 multiply_bitcast_fusion
  36.5 2.3 %reduce-window.6 = f32[8,4,2,128]{3,0,1,2:T(8,128)S(1)} reduce-window(f32[8,4,2,128]{3,0,1,2:T(8,128)S(1)} %copy.49, f32[]{:T(128)} %constant.30.clone.1), window={size=1x1x1x128 pad=0_0x0_0x0_0x127_0}, to_apply=%region_0.1 | reduce-window | flops 1040384 | bytes 65540 | tf_op jit(solution)/shard_map/reduce-window
  38.8 0.2 slice_reduce_fusion
  39.0 0.1 copy_bitcast_fusion
  39.1 0.2 slice_reduce_fusion.5
  39.2 0.2 reduce_window_sum.36
  39.4 0.1 fusion.40
  39.6 20.6 %all-to-all-done = bf16[128,16,256]{0,2,1:T(8,128)(2,1)S(1)} async-done(((bf16[128,16,256]{0,2,1:T(8,128)(2,1)}), bf16[128,16,256]{0,2,1:T(8,128)(2,1)S(1)}, u32[]{:S(2)}, u32[]{:S(2)}) %all-to-all-start) | async-done | bytes 1048608 | tf_op jit(solution)/shard_map/all_to_all | solution.py:88
  60.2 0.7 copy.47
  60.9 0.6 reshape_reshape.3
  61.5 22.5 %all-gather.2.cloned.1.call-done = bf16[2048,256]{0,1:T(8,128)(2,1)} async-done(((bf16[128,256]{0,1:T(8,128)(2,1)}), bf16[2048,256]{0,1:T(8,128)(2,1)}) %all-gather.2.cloned.1.call-update) | async-done | bytes 1048592 | tf_op jit(solution)/shard_map/all_gather | solution.py:91
  84.0 2.1 %fusion.41 = (bf16[2048,128]{0,1:T(8,128)(2,1)S(1)}, bf16[2048,128]{0,1:T(8,128)(2,1)}) fusion(bf16[2048,256]{0,1:T(8,128)(2,1)} %all-gather.2.cloned.1.call-done), kind=kLoop, calls=%fused_computation.71 | loop fusion | bytes 2097152 | tf_op jit(solution)/shard_map/slice | solution.py:105
  86.0 0.3 copy.54
  86.3 1.3 copy.53
  87.6 0.2 convert_multiply_fusion.1
  87.8 1.6 %fusion.21 = f32[8,4,64,128]{3,2,1,0:T(8,128)S(1)} fusion(bf16[8,256,128,1]{2,1,3,0:T(8,128)(2,1)S(1)} %bitcast.72, f32[8,256,4,64]{1,0,3,2:T(8,128)S(1)} %convert_multiply_fusion.1), kind=kOutput, calls=%fused_computation.31 | convolution fusion | flops 805306368 | bytes 3670016 | tf_op jit(solution)/shard_map/cshp,csn->chpn/dot_general | solution.py:58
  89.5 1.6 %convolution_bitcast_fusion = f32[8,4,64,128]{3,0,2,1:T(8,128)S(1)} fusion(f32[8,4,64,128]{3,2,1,0:T(8,128)S(1)} %fusion.21, f32[4,8]{1,0:T(4,128)S(1)} %bitcast.76, f32[4,8]{1,0:T(4,128)S(1)} %subtract_bitcast_fusion, pred[8,8]{1,0:T(8,128)(4,1)S(1)} %iota_compare_fusion.1), kind=kOutput, calls=%fused_computation.36 | convolution fusion | flops 25166336 | bytes 2097472 | tf_op jit(solution)/shard_map/hcd,dhpn->chpn/dot_general | solution.py:62
  91.1 1.0 fusion.25
  92.1 0.4 fusion.43
  92.5 6.2 %bitcast_add_fusion = f32[8,256,4,64]{1,3,2,0:T(8,128)S(1)} fusion(f32[8,256,4,64]{1,3,2,0:T(8,128)S(1)} %fusion.25, f32[8,4,256]{2,1,0:T(4,128)S(1)} %copy.55, f32[8,256,256]{2,1,0:T(8,128)S(1)} %fusion.43, f32[8,4,256]{2,1,0:T(4,128)S(1)} %copy.51, pred[256,256]{1,0:T(8,128)(4,1)S(1)} %iota_compare_fusion, ...), kind=kOutput, calls=%fused_computation.28 | convolution fusion | flops 1620049920 | bytes 7503872 | tf_op jit(solution)/shard_map/chts,cshp->cthp/dot_general | solution.py:55
  98.7 2.8 %copy.61 = f32[8,256,4,64]{1,0,3,2:T(8,128)} copy(f32[8,256,4,64]{1,3,2,0:T(8,128)S(1)} %bitcast_add_fusion) | data formatting | bytes 4194304 | tf_op jit(solution)/shard_map/add | solution.py:66
  101.5 1.6 %reshape.121 = f32[16,128,256]{1,0,2:T(8,128)S(1)} reshape(f32[8,256,4,64]{1,0,3,2:T(8,128)} %copy.61) | data formatting | bytes 4194304 | tf_op jit(solution)/shard_map/reshape | solution.py:66
  103.1 1.7 %fusion.20 = bf16[16,128,256]{1,2,0:T(8,128)(2,1)} fusion(f32[16,128,256]{1,0,2:T(8,128)S(1)} %reshape.121, f32[256]{0:T(256)S(1)} %mul.156, bf16[128,16,256]{0,2,1:T(8,128)(2,1)S(1)} %all-to-all-done), kind=kLoop, calls=%fused_computation.30 | loop fusion | flops 2097152 | bytes 4195328 | tf_op jit(solution)/shard_map/convert_element_type | solution.py:110
  104.8 6.6 %all-to-all-start.2 = ((bf16[16,128,256]{1,2,0:T(8,128)(2,1)}), bf16[16,128,256]{1,2,0:T(8,128)(2,1)S(1)}, u32[]{:S(2)}, u32[]{:S(2)}) async-start(bf16[16,128,256]{1,2,0:T(8,128)(2,1)} %fusion.20), calls=%async_computation.2 | async-start | bytes 2097152 | tf_op jit(solution)/shard_map/all_to_all | solution.py:111
  111.4 0.7 copy.63
  112.1 22.5 %all-to-all-done.2 = bf16[16,128,256]{1,2,0:T(8,128)(2,1)S(1)} async-done(((bf16[16,128,256]{1,2,0:T(8,128)(2,1)}), bf16[16,128,256]{1,2,0:T(8,128)(2,1)S(1)}, u32[]{:S(2)}, u32[]{:S(2)}) %all-to-all-start.2) | async-done | bytes 1048608 | tf_op jit(solution)/shard_map/all_to_all | solution.py:111
  134.6 0.7 multiply_reduce_fusion
  135.4 0.9 multiply_convert_fusion.1
  136.2 1.3 copy.64
  (27 shorter events, 0.2 us)
Async XLA Ops:
  6.5 14.4 %copy-start.3 = (f32[64]{0:T(128)S(1)}, f32[64]{0:T(128)}, u32[]{:S(2)}) copy-start(f32[64]{0:T(128)} %param.14) | copy-start | bytes 772
  6.5 24.3 %all-to-all-start.1 = ((bf16[128,16,4]{0,2,1:T(4,128)(2,1)}), bf16[128,16,4]{0,2,1:T(4,128)(2,1)S(1)}, u32[]{:S(2)}, u32[]{:S(2)}) async-start(bf16[128,16,4]{0,2,1:T(4,128)(2,1)} %bitcast.77), calls=%async_computation.1 | async-start | bytes 32768 | tf_op jit(solution)/shard_map/all_to_all | solution.py:89
  13.7 70.3 %all-gather.2.cloned.1.call-start = ((), (), s32[]{:S(2)}) async-start(), calls=%async_computation.3 | async-start | bytes 1114112 | tf_op jit(solution)/shard_map/all_gather | solution.py:91
  14.6 7.6 %collective-permute-start = (bf16[3,4352]{1,0:T(4,128)(2,1)S(1)}, bf16[3,4352]{1,0:T(4,128)(2,1)S(1)}, u32[]{:S(2)}, u32[]{:S(2)}) collective-permute-start(bf16[3,4352]{1,0:T(4,128)(2,1)S(1)} %slice.49), channel_id=1, source_target_pairs={{0,2},{2,4},{4,6},{6,8},{8,10},{10,12},{12,14},{14,16},{16,18},{18... | collective-permute-start | bytes 78344 | tf_op jit(solution)/shard_map/ppermute | solution.py:15
  22.8 0.8 copy-start.1
  29.1 6.9 %copy-start.4 = (f32[64]{0:T(128)S(1)}, f32[64]{0:T(128)}, u32[]{:S(2)}) copy-start(f32[64]{0:T(128)} %param.15) | copy-start | bytes 772
  29.1 6.9 %copy-start.5 = (f32[64]{0:T(128)S(1)}, f32[64]{0:T(128)}, u32[]{:S(2)}) copy-start(f32[64]{0:T(128)} %param.16) | copy-start | bytes 772
  30.9 29.3 %all-to-all-start = ((bf16[128,16,256]{0,2,1:T(8,128)(2,1)}), bf16[128,16,256]{0,2,1:T(8,128)(2,1)S(1)}, u32[]{:S(2)}, u32[]{:S(2)}) async-start(bf16[128,16,256]{0,2,1:T(8,128)(2,1)} %bitcast), calls=%async_computation | async-start | bytes 2097152 | tf_op jit(solution)/shard_map/all_to_all | solution.py:88
  104.8 6.6 %copy-start = (bf16[128,4096]{1,0:T(8,128)(2,1)S(1)}, bf16[128,4096]{1,0:T(8,128)(2,1)}, u32[]{:S(2)}) copy-start(bf16[128,4096]{1,0:T(8,128)(2,1)} %param.10) | copy-start | bytes 3145732
  104.8 29.8 %all-to-all-start.2 = ((bf16[16,128,256]{1,2,0:T(8,128)(2,1)}), bf16[16,128,256]{1,2,0:T(8,128)(2,1)S(1)}, u32[]{:S(2)}, u32[]{:S(2)}) async-start(bf16[16,128,256]{1,2,0:T(8,128)(2,1)} %fusion.20), calls=%async_computation.2 | async-start | bytes 2097152 | tf_op jit(solution)/shard_map/all_to_all | solution.py:111
  111.4 23.9 %copy-start.2 = (f32[4096]{0:T(1024)S(1)}, f32[4096]{0:T(1024)}, u32[]{:S(2)}) copy-start(f32[4096]{0:T(1024)} %param.17) | copy-start | bytes 49156
Sparse Core Ops, SparseCore 0:
  31.0 52.9 all-gather.1
where the time goes:
time: 147 us; the launch traced here: 144 us
  waiting for transfers between devices  66.8 us (45%)
  starting transfers between devices  22.3 us (15%)
  local copies, waits for them, and re-layouts  18.1 us (12%)
  between operations  13.7 us (9%)
  other arithmetic  12.6 us (9%)
  matrix products  10.8 us (7%)
    all_gather x1, waiting for transfers between devices, shards(): lax.all_gather(activated[:, inner_width:], 'seq', axis=0, tiled=True)  22.5 us
    all_to_all x1, waiting for transfers between devices, shards(): lax.all_to_all(head_output, 'seq', split_axis=0, concat_axis=1, tiled=True)  22.5 us
    all_to_all x1, waiting for transfers between devices, shards(): lax.all_to_all(activated[:, :inner_width], 'seq', split_axis=1, concat_ax...  20.6 us
    all_to_all x1, starting transfers between devices, shards(): lax.all_to_all(step_input, 'seq', split_axis=1, concat_axis=0, tiled=True)  7.13 us
    all_to_all x1, starting transfers between devices, shards(): lax.all_to_all(head_output, 'seq', split_axis=0, concat_axis=1, tiled=True)  6.59 us
    dot_general x1, matrix products, dual_form(): jnp.einsum('chts,cshp->cthp', mixing, block_values, precision=highest)  6.18 us
    convert_element_type x1, other arithmetic, convolve(): return jax.nn.silu(mixed).astype(jnp.bfloat16)  5.49 us
    all_to_all x1, starting transfers between devices, shards(): lax.all_to_all(activated[:, :inner_width], 'seq', split_axis=1, concat_ax...  5.13 us
  transfers between devices with their start and end apart: 5, of which 4 were waited for; matrix products, arithmetic and copies ran while one was open for 12% of the time, Pallas kernels for 0%

commit v1 on v0

v1 whole, which is shorter than its diff:
```python
import functools
import jax
import jax.numpy as jnp
from jax import lax
from jax.experimental import pallas as pl
from jax.experimental.pallas import tpu as pltpu
from jax.sharding import PartitionSpec as P

HEADDIM = 64
STATE = 128
HEADS = 64
GROUP = 4
PARTS = 4
EXTRA = 16
MESH = pl.DeviceIdType.MESH


def shifted(value, axis, steps):
    count = lax.axis_size(axis)
    initial, last = (max(0, -steps), min(count, count - steps))
    return lax.ppermute(value, axis, [(source, source + steps) for source in range(initial, last)])


def convolve(conv_input, conv_weight, convolution_bias):
    tap_count = conv_weight.shape[0]
    row_count = conv_input.shape[0]
    earlier = shifted(conv_input[row_count - (tap_count - 1) :], "seq", 1)
    padded = jnp.concatenate([earlier, conv_input], axis=0).astype(jnp.float32)
    mixed = convolution_bias[None, :]
    for offset in range(tap_count):
        mixed = mixed + conv_weight[offset][None, :] * padded[offset : offset + row_count]
    return jax.nn.silu(mixed).astype(jnp.bfloat16)


def prefix_kernel(
    count, group, s_ref, f_ref, got, ein, eout, fsend, gsum,
    send_a, recv_a, send_c, recv_c, send_f, recv_f,
):
    rows = ein.shape[0]
    width = ein.shape[1]
    part = width // PARTS
    planes = count // group
    me = lax.axis_index("seq")
    mine = lax.rem(me, group)
    plane = me // group
    base = plane * group
    has_prev = plane > 0
    has_next = plane < planes - 1
    before = jnp.maximum(me - group, 0)
    after = jnp.minimum(me + group, count - 1)

    barrier = pltpu.get_barrier_semaphore()
    for step in range(1, group):
        other = base + lax.rem(mine + step, group)
        pl.semaphore_signal(barrier, inc=1, device_id={"seq": other}, device_id_type=MESH)

    @pl.when(has_prev)
    def _():
        pl.semaphore_signal(barrier, inc=1, device_id={"seq": before}, device_id_type=MESH)

    @pl.when(has_next)
    def _():
        pl.semaphore_signal(barrier, inc=1, device_id={"seq": after}, device_id_type=MESH)

    peers = group - 1 + jnp.minimum(plane, 1) + jnp.minimum(planes - 1 - plane, 1)
    pl.semaphore_wait(barrier, peers)

    def share(step):
        member = lax.rem(mine + step, group)
        return pltpu.make_async_remote_copy(
            src_ref=s_ref.at[:, pl.ds(pl.multiple_of(member * width, width), width)],
            dst_ref=got.at[step],
            send_sem=send_a.at[step],
            recv_sem=recv_a.at[step],
            device_id={"seq": base + member},
            device_id_type=MESH,
        )

    def chain(k):
        columns = pl.ds(k * part, part)
        return pltpu.make_async_remote_copy(
            src_ref=eout.at[:, columns],
            dst_ref=ein.at[:, columns],
            send_sem=send_c.at[k],
            recv_sem=recv_c.at[k],
            device_id={"seq": after},
            device_id_type=MESH,
        )

    def back(step, k):
        member = lax.rem(mine + step, group)
        own = pl.ds(pl.multiple_of(mine * width + k * part, part), part)
        return pltpu.make_async_remote_copy(
            src_ref=fsend.at[step, :, pl.ds(k * part, part)],
            dst_ref=f_ref.at[:, own],
            send_sem=send_f.at[step, k],
            recv_sem=recv_f.at[step, k],
            device_id={"seq": base + member},
            device_id_type=MESH,
        )

    for step in range(1, group):
        share(step).start()
    got[0] = s_ref[:, pl.ds(pl.multiple_of(mine * width, width), width)]
    for step in range(1, group):
        share(step).wait_recv()

    slots = [lax.rem(mine - i + group, group) for i in range(group)]
    marks = []
    for k in range(PARTS):
        columns = pl.ds(k * part, part)
        running = jnp.zeros((rows, part), jnp.float32)
        level = jnp.zeros((1, part), jnp.float32)
        levels = [level]
        for i in range(group):
            tail = got[slots[i], rows : rows + EXTRA, columns].astype(jnp.float32)
            step_log = tail[0:1] + tail[1:2] + tail[2:3]
            running = jnp.exp(step_log) * running + got[slots[i], :rows, columns].astype(jnp.float32)
            gsum[i, :, columns] = running
            level = level + step_log
            levels.append(level)
        marks.append(levels)

    for k in range(PARTS):
        columns = pl.ds(k * part, part)
        levels = marks[k]

        @pl.when(has_prev)
        def _():
            chain(k).wait_recv()

        @pl.when(jnp.logical_not(has_prev))
        def _():
            ein[:, columns] = jnp.zeros((rows, part), jnp.bfloat16)

        entering = ein[:, columns].astype(jnp.float32)

        @pl.when(has_next)
        def _():
            eout[:, columns] = (jnp.exp(levels[group]) * entering + gsum[group - 1, :, columns]).astype(jnp.bfloat16)
            chain(k).start()

        for j in range(group):
            if j == 0:
                value = entering
            else:
                value = jnp.exp(levels[j]) * entering + gsum[j - 1, :, columns]
            fsend[lax.rem(j - mine + group, group), :, columns] = value.astype(jnp.bfloat16)
        for step in range(1, group):
            back(step, k).start()
        own = pl.ds(pl.multiple_of(mine * width + k * part, part), part)
        f_ref[:, own] = fsend[0, :, columns]

    for step in range(1, group):
        share(step).wait_send()
    for k in range(PARTS):
        @pl.when(has_next)
        def _():
            chain(k).wait_send()

        for step in range(1, group):
            back(step, k).wait_send()
            source = lax.rem(mine - step + group, group)
            landed = pl.ds(pl.multiple_of(source * width + k * part, part), part)
            pltpu.make_async_remote_copy(
                src_ref=fsend.at[step, :, pl.ds(k * part, part)],
                dst_ref=f_ref.at[:, landed],
                send_sem=send_f.at[step, k],
                recv_sem=recv_f.at[step, k],
                device_id={"seq": base + lax.rem(mine + step, group)},
                device_id_type=MESH,
            ).wait_recv()


def entering_states(packed):
    count = lax.axis_size("seq")
    group = GROUP if count % GROUP == 0 else 1
    rows = packed.shape[0] - EXTRA
    width = packed.shape[1] // group
    return pl.pallas_call(
        functools.partial(prefix_kernel, count, group),
        out_shape=jax.ShapeDtypeStruct((rows, packed.shape[1]), jnp.bfloat16),
        in_specs=[pl.BlockSpec(memory_space=pltpu.VMEM)],
        out_specs=pl.BlockSpec(memory_space=pltpu.VMEM),
        scratch_shapes=[
            pltpu.VMEM((group, rows + EXTRA, width), jnp.bfloat16),
            pltpu.VMEM((rows, width), jnp.bfloat16),
            pltpu.VMEM((rows, width), jnp.bfloat16),
            pltpu.VMEM((group, rows, width), jnp.bfloat16),
            pltpu.VMEM((group, rows, width), jnp.float32),
            pltpu.SemaphoreType.DMA((group,)),
            pltpu.SemaphoreType.DMA((group,)),
            pltpu.SemaphoreType.DMA((PARTS,)),
            pltpu.SemaphoreType.DMA((PARTS,)),
            pltpu.SemaphoreType.DMA((group, PARTS)),
            pltpu.SemaphoreType.DMA((group, PARTS)),
        ],
        compiler_params=pltpu.CompilerParams(
            collective_id=0, has_side_effects=True, vmem_limit_bytes=32 * 1024 * 1024
        ),
    )(packed)


def split(value):
    high = value.astype(jnp.bfloat16)
    low = (value - high.astype(jnp.float32)).astype(jnp.bfloat16)
    return high, low


def mix_kernel(act, entering, gate, cols, rows_ref, steps, skip, gain, out, mixed):
    tokens = act.shape[0]
    inner = entering.shape[1]
    block = 8 * HEADDIM
    b_rows = act[:, inner : inner + STATE]
    c_rows = act[:, inner + STATE : inner + 2 * STATE]
    scores = lax.dot_general(c_rows, b_rows, (((1,), (1,)), ((), ())), preferred_element_type=jnp.float32)
    lower = lax.broadcasted_iota(jnp.int32, (tokens, tokens), 0) >= lax.broadcasted_iota(jnp.int32, (tokens, tokens), 1)
    scores = jnp.where(lower, scores, 0.0)
    c_wide = c_rows.astype(jnp.float32)
    first = lax.broadcasted_iota(jnp.int32, (tokens, 2 * HEADDIM), 1) < HEADDIM

    def body(g, carry):
        for pair in range(4):
            columns = pl.ds(pl.multiple_of(g * block + pair * 128, 128), 128)
            x = act[:, columns]
            stacked = jnp.concatenate([x, entering[:, columns]], axis=0)
            halves = []
            for half in range(2):
                h = pair * 2 + half
                col = cols[g, :, h : h + 1]
                row = rows_ref[g, h : h + 1, :]
                inside = jnp.exp(jnp.where(lower, col - row, -1e30)) * scores * steps[g, h : h + 1, :]
                whole = jnp.concatenate([inside, jnp.exp(col) * c_wide], axis=1)
                high, low = split(whole)
                halves.append(
                    jnp.dot(high, stacked, preferred_element_type=jnp.float32)
                    + jnp.dot(low, stacked, preferred_element_type=jnp.float32)
                )
            result = jnp.where(first, halves[0], halves[1]) + skip[:, columns] * x.astype(jnp.float32)
            mixed[:, columns] = result.astype(jnp.bfloat16)
        return carry

    lax.fori_loop(0, inner // block, body, 0)

    def norm(r, carry):
        take = pl.ds(pl.multiple_of(r * 16, 16), 16)
        z = gate[take, :].astype(jnp.float32)
        gated = mixed[take, :].astype(jnp.float32) * (z / (1.0 + jnp.exp(-z)))
        spread = jnp.mean(gated * gated, axis=-1, keepdims=True)
        out[take, :] = (gated * lax.rsqrt(spread + 1e-05) * gain[...]).astype(jnp.bfloat16)
        return carry

    lax.fori_loop(0, tokens // 16, norm, 0)


def shards(
    conv_input, gate_input, step_input, conv_weight, convolution_bias,
    step_bias, decay_log, skip_gain, norm_gain,
):
    highest = lax.Precision.HIGHEST
    inner = HEADS * HEADDIM
    tokens = conv_input.shape[0]
    activated = convolve(conv_input, conv_weight, convolution_bias)
    step_size = jax.nn.softplus(step_input.astype(jnp.float32) + step_bias[None, :])
    rate = -jnp.exp(decay_log)
    lower = (jnp.arange(tokens)[:, None] >= jnp.arange(tokens)[None, :]).astype(jnp.float32)
    within = jnp.dot(lower, step_size * rate[None, :], precision=highest)
    ends = within[-1]
    tail = jnp.repeat(jnp.exp(ends[None, :] - within) * step_size, HEADDIM, axis=1)
    weighted = (tail * activated[:, :inner].astype(jnp.float32)).astype(jnp.bfloat16)
    state = lax.dot_general(
        activated[:, inner : inner + STATE], weighted, (((0,), (0,)), ((), ())),
        preferred_element_type=jnp.float32,
    ).astype(jnp.bfloat16)
    high = lax.reduce_precision(ends, 8, 7)
    middle = lax.reduce_precision(ends - high, 8, 7)
    low = lax.reduce_precision(ends - high - middle, 8, 7)
    logs = jnp.repeat(jnp.stack([high, middle, low]), HEADDIM, axis=1).astype(jnp.bfloat16)
    packed = jnp.concatenate([state, logs, jnp.zeros((EXTRA - 3, inner), jnp.bfloat16)], axis=0)
    entering = entering_states(packed)
    groups = HEADS // 8
    cols = jnp.transpose(within.reshape(tokens, groups, 8), (1, 0, 2))
    rows = jnp.transpose(within).reshape(groups, 8, tokens)
    steps = jnp.transpose(step_size).reshape(groups, 8, tokens)
    skip = jnp.repeat(skip_gain, HEADDIM)[None, :]
    return pl.pallas_call(
        mix_kernel,
        out_shape=jax.ShapeDtypeStruct((tokens, inner), jnp.bfloat16),
        in_specs=[pl.BlockSpec(memory_space=pltpu.VMEM)] * 8,
        out_specs=pl.BlockSpec(memory_space=pltpu.VMEM),
        scratch_shapes=[pltpu.VMEM((tokens, inner), jnp.bfloat16)],
        compiler_params=pltpu.CompilerParams(vmem_limit_bytes=32 * 1024 * 1024),
    )(activated, entering, gate_input, cols, rows, steps, skip, norm_gain[None, :])


def solution(mesh):
    in_specs = (
        P(("doc", "seq"), None),
        P(("doc", "seq"), None),
        P(("doc", "seq"), None),
        P(), P(), P(), P(), P(), P(),
    )
    out_specs = P(("doc", "seq"), None)
    return jax.shard_map(shards, mesh=mesh, in_specs=in_specs, out_specs=out_specs, check_vma=False)
```

time: 147 us -> 60.3 us (0.41); the launches traced: 144 us -> 59.2 us
  waiting for transfers between devices: 66.8 us -> 0.01 us
  Pallas kernels: 0 us -> 43.1 us
  starting transfers between devices: 22.3 us -> 3.4 us
  between operations: 13.7 us -> 0.16 us
  local copies, waits for them, and re-layouts: 18.1 us -> 6.35 us
  matrix products: 10.8 us -> 1.5 us
  other arithmetic: 12.6 us -> 4.71 us
    pallas_call x0 -> x2, Pallas kernels: none -> 43.1 us  [the longest x1 35.8 us: entering_states(): pl.pallas_call(functools.partial(prefix_kernel, count, group), out_shape=...]
    all_to_all x3 -> x0, waiting for transfers between devices: 43.1 us -> none  [the longest x1 22.5 us: shards(): lax.all_to_all(head_output, 'seq', split_axis=0, concat_axis=1, tiled=True)]
    all_gather x1 -> x0, waiting for transfers between devices: 22.5 us -> none  [shards(): lax.all_gather(activated[:, inner_width:], 'seq', axis=0, tiled=True)]
    all_to_all x3 -> x0, starting transfers between devices: 18.9 us -> none  [the longest x1 7.13 us: shards(): lax.all_to_all(step_input, 'seq', split_axis=1, concat_axis=0, tiled=True)]
    dot_general x5 -> x2, matrix products: 10.8 us -> 1.5 us  [the longest x1 0.99 us: shards(): within = jnp.dot(lower, step_size * rate[None, :], precision=highest)]
    slice x7 -> x1, local copies, waits for them, and re-layouts: 5.64 us -> 0.07 us  [shards(): ends = within[-1]]
    convert_element_type x1, other arithmetic: 5.49 us -> 1.42 us  [convolve(): return jax.nn.silu(mixed).astype(jnp.bfloat16)]
    add x1 -> x0, local copies, waits for them, and re-layouts: 2.79 us -> none  [dual_form(): result = (inside + outside).reshape(row_count, head_count, head_width)]
  transfers between devices with their start and end apart: 5 -> 1, of which waited for: 4 -> 0; matrix products, arithmetic and copies ran while one was open for 12% -> 13% of each run, Pallas kernels for 0% -> 0%
where the time goes in v1:
time: 60.3 us; the launch traced here: 59.2 us
  Pallas kernels  43.1 us (71%)
  local copies, waits for them, and re-layouts  6.35 us (11%)
  other arithmetic  4.71 us (8%)
  starting transfers between devices  3.4 us (6%)
  matrix products  1.5 us (2%)
    pallas_call x1, Pallas kernels, entering_states(): pl.pallas_call(functools.partial(prefix_kernel, count, group), out_shape=...  35.8 us
    pallas_call x1, Pallas kernels, shards(): pl.pallas_call(mix_kernel, out_shape=jax.ShapeDtypeStruct((tokens, inner)...  7.3 us
    ppermute x1, starting transfers between devices, shifted(): lax.ppermute(value, axis, [(source, source + steps) for source in range(i...  3.4 us
    reshape x1, local copies, waits for them, and re-layouts, shards(): jnp.repeat(jnp.exp(ends[None, :] - within) * step_size, HEADDIM, axis=1)  1.93 us
    convert_element_type x1, other arithmetic, convolve(): padded = jnp.concatenate([earlier, conv_input], axis=0).astype(jnp.float32)  1.49 us
    broadcast_in_dim x1, local copies, waits for them, and re-layouts, shards(): jnp.repeat(jnp.exp(ends[None, :] - within) * step_size, HEADDIM, axis=1)  1.49 us
    convert_element_type x1, other arithmetic, convolve(): return jax.nn.silu(mixed).astype(jnp.bfloat16)  1.42 us
    slice x1, local copies, waits for them, and re-layouts, convolve(): conv_weight[offset][None, :] * padded[offset:offset + row_count]  1.24 us
  transfers between devices with their start and end apart: 1, of which 0 were waited for; matrix products, arithmetic and copies ran while one was open for 13% of the time, Pallas kernels for 0%

profile of v1, /device:TPU:24, one launch (start us, length us, event | category | flops | bytes accessed | tf_op | source)
XLA Modules:
  0.0 59.2 jit_solution(12484689825194758719)
XLA Ops:
  0.0 0.9 %slice.37 = bf16[3,4352]{1,0:T(4,128)(2,1)S(1)} slice(bf16[128,4352]{1,0:T(8,128)(2,1)} %param.9), slice={[125:128], [0:4352]} | slice | bytes 52224 | tf_op jit(solution)/shard_map/slice | solution.py:27
  0.9 3.4 %collective-permute-start = (bf16[3,4352]{1,0:T(4,128)(2,1)S(1)}, bf16[3,4352]{1,0:T(4,128)(2,1)S(1)}, u32[]{:S(2)}, u32[]{:S(2)}) collective-permute-start(bf16[3,4352]{1,0:T(4,128)(2,1)S(1)} %slice.37), channel_id=1, source_target_pairs={{0,2},{2,4},{4,6},{6,8},{8,10},{10,12},{12,14},{14,16},{16,18},{18... | collective-permute-start | bytes 78344 | tf_op jit(solution)/shard_map/ppermute | solution.py:21
  4.3 1.2 %slice_reduce_fusion.3 = (f32[4352]{0:T(1024)S(1)}, f32[4352]{0:T(1024)S(1)}, f32[4352]{0:T(1024)S(1)}, f32[4352]{0:T(1024)S(1)}) fusion(f32[4,4352]{1,0:T(4,128)} %param.12), kind=kLoop, calls=%fused_computation.23 | loop fusion | bytes 139264 | tf_op jit(solution)/shard_map/slice | solution.py:31
  5.6 0.7 %exponential_negate_fusion = f32[64]{0:T(128)S(1)} fusion(f32[64]{0:T(128)} %param.15), kind=kLoop, calls=%fused_computation.32 | loop fusion | flops 64 | bytes 512 | tf_op jit(solution)/shard_map/neg | solution.py:265
  6.2 1.0 %fusion.5 = f32[128,64]{0,1:T(8,128)S(1)} fusion(f32[64]{0:T(128)S(1)} %exponential_negate_fusion, bf16[128,64]{0,1:T(8,128)(2,1)} %param.11, f32[64]{0:T(128)} %param.14), kind=kOutput, calls=%fused_computation.16 | convolution fusion | flops 12673024 | bytes 49664 | tf_op jit(solution)/shard_map/dot_general | solution.py:267
  7.2 0.1 slice.53
  7.3 0.1 copy.23
  7.4 0.8 %fusion.11 = (f32[8,8,128]{2,1,0:T(8,128)S(1)}, f32[128,64]{0,1:T(8,128)S(1)}) fusion(f32[64]{0:T(128)} %param.14, bf16[128,64]{0,1:T(8,128)(2,1)} %param.11, f32[128,64]{0,1:T(8,128)S(1)} %fusion.5, f32[64]{0:T(128)S(1)} %bitcast.17), kind=kLoop, calls=%fused_computation.33 | loop fusion | flops 81920 | bytes 115200 | tf_op jit(solution)/shard_map/reshape | solution.py:284
  8.2 1.5 %broadcast_in_dim.20 = f32[128,64,64]{0,2,1:T(8,128)} broadcast(f32[128,64]{0,1:T(8,128)S(1)} %get-tuple-element.10), dimensions={0,1} | broadcast | bytes 2129920 | tf_op jit(solution)/shard_map/broadcast_in_dim | solution.py:269
  9.7 0.0 copy-start.3
  9.7 1.9 %copy.21 = f32[128,4096]{1,0:T(8,128)S(1)} copy(f32[128,4096]{0,1:T(8,128)} %bitcast.16) | data formatting | bytes 4194304 | tf_op jit(solution)/shard_map/reshape | solution.py:269
  11.7 0.0 copy-start.2
  11.7 0.1 broadcast_in_dim.21
  11.8 0.1 convert_element_type.30
  11.9 0.2 copy.22
  12.1 0.0 copy-done.3
  12.1 0.1 broadcast_in_dim.23
  12.2 0.1 broadcast_in_dim_reshape.3.skip
  12.3 0.1 pad.2.clone
  12.3 0.0 collective-permute-done
  12.4 1.5 %maximum_convert_fusion = f32[131,4352]{1,0:T(8,128)S(1)} fusion(bf16[128,4352]{1,0:T(8,128)(2,1)} %param.9, bf16[3,4352]{1,0:T(4,128)(2,1)S(1)} %collective-permute-done), kind=kLoop, calls=%fused_computation.11 | loop fusion | flops 2280448 | bytes 3420672 | tf_op jit(solution)/shard_map/convert_element_type | solution.py:28
  13.8 0.0 copy-done.2
  13.9 1.4 %multiply_convert_fusion.act = bf16[128,4352]{1,0:T(8,128)(2,1)S(1)} fusion(f32[131,4352]{1,0:T(8,128)S(1)} %maximum_convert_fusion, f32[4352]{0:T(1024)S(1)} %get-tuple-element.7, f32[4352]{0:T(1024)S(1)} %get-tuple-element.8, f32[4352]{0:T(1024)S(1)} %get-tuple-element.6, f32[4352]{0:T(1024)S(1)} %get-tuple-element.5, f32[4352]{0:T(1024)S(1)} %copy-done.2), kind=kLoop, calls=%fused_computation.9 | loop fusion | flops 7241728 | bytes 10114048 | tf_op jit(solution)/shard_map/convert_element_type | solution.py:32
  15.3 0.5 convolution_convert_fusion
  15.8 0.0 copy-start
  15.8 0.0 copy-start.1
  15.8 0.3 maximum_maximum_fusion.s_ref
  16.1 35.8 %shard_map.91.entering = bf16[128,4096]{1,0:T(8,128)(2,1)S(1)} custom-call(bf16[144,4096]{1,0:T(8,128)(2,1)S(1)} %maximum_maximum_fusion.s_ref), custom_call_target="tpu_custom_call" | custom-call | tf_op jit(solution)/shard_map/pallas_call | solution.py:180
  51.9 0.0 copy-done
  51.9 0.0 copy-done.1
  51.9 7.3 %shard_map.92 = bf16[128,4096]{1,0:T(8,128)(2,1)} custom-call(bf16[128,4352]{1,0:T(8,128)(2,1)S(1)} %multiply_convert_fusion.act, bf16[128,4096]{1,0:T(8,128)(2,1)S(1)} %shard_map.91.entering, bf16[128,4096]{1,0:T(8,128)(2,1)S(1)} %copy-done, f32[8,128,8]{2,1,0:T(8,128)S(1)} %bitcast.12, f32[8,8,128]{2,1,0:T(8,128)S(1)} %bitcast.14, ...), custom_call_target="tpu_custom_call" | custom-call | tf_op jit(solution)/shard_map/pallas_call | solution.py:286
  (3 shorter events, 0.0 us)
Async XLA Ops:
  0.9 11.4 %collective-permute-start = (bf16[3,4352]{1,0:T(4,128)(2,1)S(1)}, bf16[3,4352]{1,0:T(4,128)(2,1)S(1)}, u32[]{:S(2)}, u32[]{:S(2)}) collective-permute-start(bf16[3,4352]{1,0:T(4,128)(2,1)S(1)} %slice.37), channel_id=1, source_target_pairs={{0,2},{2,4},{4,6},{6,8},{8,10},{10,12},{12,14},{14,16},{16,18},{18... | collective-permute-start | bytes 78344 | tf_op jit(solution)/shard_map/ppermute | solution.py:21
  9.7 2.4 %copy-start.3 = (f32[64]{0:T(128)S(1)}, f32[64]{0:T(128)}, u32[]{:S(2)}) copy-start(f32[64]{0:T(128)} %param.16) | copy-start | bytes 772
  11.7 2.2 %copy-start.2 = (f32[4352]{0:T(1024)S(1)}, f32[4352]{0:T(1024)}, u32[]{:S(2)}) copy-start(f32[4352]{0:T(1024)} %param.13) | copy-start | bytes 52228
  15.8 36.1 %copy-start = (bf16[128,4096]{1,0:T(8,128)(2,1)S(1)}, bf16[128,4096]{1,0:T(8,128)(2,1)}, u32[]{:S(2)}) copy-start(bf16[128,4096]{1,0:T(8,128)(2,1)} %gate.1) | copy-start | bytes 3145732
  15.8 36.1 %copy-start.1 = (f32[4096]{0:T(1024)S(1)}, f32[4096]{0:T(1024)}, u32[]{:S(2)}) copy-start(f32[4096]{0:T(1024)} %param.17) | copy-start | bytes 49156

commit v2 on v1

--- a/solution.py
+++ b/solution.py
@@ -65,13 +65,13 @@
     peers = group - 1 + jnp.minimum(plane, 1) + jnp.minimum(planes - 1 - plane, 1)
     pl.semaphore_wait(barrier, peers)
 
-    def share(step):
+    def share(step, k):
         member = lax.rem(mine + step, group)
         return pltpu.make_async_remote_copy(
-            src_ref=s_ref.at[:, pl.ds(pl.multiple_of(member * width, width), width)],
-            dst_ref=got.at[step],
-            send_sem=send_a.at[step],
-            recv_sem=recv_a.at[step],
+            src_ref=s_ref.at[:, pl.ds(pl.multiple_of(member * width + k * part, part), part)],
+            dst_ref=got.at[step, :, pl.ds(k * part, part)],
+            send_sem=send_a.at[step, k],
+            recv_sem=recv_a.at[step, k],
             device_id={"seq": base + member},
             device_id_type=MESH,
         )
@@ -99,16 +99,16 @@
             device_id_type=MESH,
         )
 
-    for step in range(1, group):
-        share(step).start()
+    for k in range(PARTS):
+        for step in range(1, group):
+            share(step, k).start()
     got[0] = s_ref[:, pl.ds(pl.multiple_of(mine * width, width), width)]
-    for step in range(1, group):
-        share(step).wait_recv()
 
     slots = [lax.rem(mine - i + group, group) for i in range(group)]
-    marks = []
     for k in range(PARTS):
         columns = pl.ds(k * part, part)
+        for step in range(1, group):
+            share(step, k).wait_recv()
         running = jnp.zeros((rows, part), jnp.float32)
         level = jnp.zeros((1, part), jnp.float32)
         levels = [level]
@@ -119,11 +119,6 @@
             gsum[i, :, columns] = running
             level = level + step_log
             levels.append(level)
-        marks.append(levels)
-
-    for k in range(PARTS):
-        columns = pl.ds(k * part, part)
-        levels = marks[k]
 
         @pl.when(has_prev)
         def _():
@@ -151,9 +146,10 @@
         own = pl.ds(pl.multiple_of(mine * width + k * part, part), part)
         f_ref[:, own] = fsend[0, :, columns]
 
-    for step in range(1, group):
-        share(step).wait_send()
     for k in range(PARTS):
+        for step in range(1, group):
+            share(step, k).wait_send()
+
         @pl.when(has_next)
         def _():
             chain(k).wait_send()
@@ -188,8 +184,8 @@
             pltpu.VMEM((rows, width), jnp.bfloat16),
             pltpu.VMEM((group, rows, width), jnp.bfloat16),
             pltpu.VMEM((group, rows, width), jnp.float32),
-            pltpu.SemaphoreType.DMA((group,)),
-            pltpu.SemaphoreType.DMA((group,)),
+            pltpu.SemaphoreType.DMA((group, PARTS)),
+            pltpu.SemaphoreType.DMA((group, PARTS)),
             pltpu.SemaphoreType.DMA((PARTS,)),
             pltpu.SemaphoreType.DMA((PARTS,)),
             pltpu.SemaphoreType.DMA((group, PARTS)),
@@ -266,7 +262,14 @@
     lower = (jnp.arange(tokens)[:, None] >= jnp.arange(tokens)[None, :]).astype(jnp.float32)
     within = jnp.dot(lower, step_size * rate[None, :], precision=highest)
     ends = within[-1]
-    tail = jnp.repeat(jnp.exp(ends[None, :] - within) * step_size, HEADDIM, axis=1)
+    spread = (jnp.arange(inner)[None, :] // HEADDIM == jnp.arange(HEADS)[:, None]).astype(jnp.bfloat16)
+    tail = jnp.exp(ends[None, :] - within) * step_size
+    top = lax.reduce_precision(tail, 8, 7)
+    tail = jnp.dot(
+        jnp.concatenate([top, tail - top], axis=1).astype(jnp.bfloat16),
+        jnp.concatenate([spread, spread], axis=0),
+        preferred_element_type=jnp.float32,
+    )
     weighted = (tail * activated[:, :inner].astype(jnp.float32)).astype(jnp.bfloat16)
     state = lax.dot_general(
         activated[:, inner : inner + STATE], weighted, (((0,), (0,)), ((), ())),
@@ -275,8 +278,9 @@
     high = lax.reduce_precision(ends, 8, 7)
     middle = lax.reduce_precision(ends - high, 8, 7)
     low = lax.reduce_precision(ends - high - middle, 8, 7)
-    logs = jnp.repeat(jnp.stack([high, middle, low]), HEADDIM, axis=1).astype(jnp.bfloat16)
-    packed = jnp.concatenate([state, logs, jnp.zeros((EXTRA - 3, inner), jnp.bfloat16)], axis=0)
+    logs = jnp.stack([high, middle, low] + [jnp.zeros_like(low)] * (EXTRA - 3)).astype(jnp.bfloat16)
+    logs = jnp.dot(logs, spread, preferred_element_type=jnp.float32).astype(jnp.bfloat16)
+    packed = jnp.concatenate([state, logs], axis=0)
     entering = entering_states(packed)
     groups = HEADS // 8
     cols = jnp.transpose(within.reshape(tokens, groups, 8), (1, 0, 2))

time: 60.3 us -> 51.2 us (0.85); the launches traced: 59.2 us -> 50.8 us
  Pallas kernels: 43.1 us -> 38.3 us
  local copies, waits for them, and re-layouts: 6.35 us -> 3.48 us
  other arithmetic: 4.71 us -> 3.43 us
    pallas_call x1, Pallas kernels: 35.8 us -> 31 us  [entering_states(): pl.pallas_call(functools.partial(prefix_kernel, count, group), out_shape=...]
    reshape x1 -> x0, local copies, waits for them, and re-layouts: 1.93 us -> none  [shards(): jnp.repeat(jnp.exp(ends[None, :] - within) * step_size, HEADDIM, axis=1)]
    broadcast_in_dim x3 -> x0, local copies, waits for them, and re-layouts: 1.58 us -> none  [the longest x1 1.49 us: shards(): jnp.repeat(jnp.exp(ends[None, :] - within) * step_size, HEADDIM, axis=1)]
    convert_element_type x1, other arithmetic: 1.49 us -> 0.24 us  [convolve(): padded = jnp.concatenate([earlier, conv_input], axis=0).astype(jnp.float32)]
    reshape x1 -> x0, other arithmetic: 0.84 us -> none  [shards(): steps = jnp.transpose(step_size).reshape(groups, 8, tokens)]
    another operation x2, other arithmetic: 0.02 us -> 0.86 us  [the longest x1 0.01 us: shards(): jnp.stack([high, middle, low])]
    broadcast_in_dim x1, local copies, waits for them, and re-layouts: 0.07 us -> 0.73 us  [shards(): skip = jnp.repeat(skip_gain, HEADDIM)[None, :]]
  transfers between devices with their start and end apart: 1 -> 1, of which waited for: 0 -> 0; matrix products, arithmetic and copies ran while one was open for 13% -> 11% of each run, Pallas kernels for 0% -> 0%
where the time goes in v2:
time: 51.2 us; the launch traced here: 50.8 us
  Pallas kernels  38.3 us (75%)
  local copies, waits for them, and re-layouts  3.48 us (7%)
  other arithmetic  3.43 us (7%)
  starting transfers between devices  3.4 us (7%)
  matrix products  2.01 us (4%)
    pallas_call x1, Pallas kernels, entering_states(): pl.pallas_call(functools.partial(prefix_kernel, count, group), out_shape=...  31 us
    pallas_call x1, Pallas kernels, shards(): pl.pallas_call(mix_kernel, out_shape=jax.ShapeDtypeStruct((tokens, inner)...  7.3 us
    ppermute x1, starting transfers between devices, shifted(): lax.ppermute(value, axis, [(source, source + steps) for source in range(i...  3.4 us
    convert_element_type x1, other arithmetic, convolve(): return jax.nn.silu(mixed).astype(jnp.bfloat16)  1.42 us
    slice x1, local copies, waits for them, and re-layouts, convolve(): conv_weight[offset][None, :] * padded[offset:offset + row_count]  1.25 us
  transfers between devices with their start and end apart: 1, of which 0 were waited for; matrix products, arithmetic and copies ran while one was open for 11% of the time, Pallas kernels for 0%

profile of v2, /device:TPU:24, one launch (start us, length us, event | category | flops | bytes accessed | tf_op | source)
XLA Modules:
  0.0 50.8 jit_solution(15507524347597626670)
XLA Ops:
  0.0 0.0 copy-start.2
  0.0 1.0 %slice.37 = bf16[3,4352]{1,0:T(4,128)(2,1)S(1)} slice(bf16[128,4352]{1,0:T(8,128)(2,1)} %param.9), slice={[125:128], [0:4352]} | slice | bytes 52224 | tf_op jit(solution)/shard_map/slice | solution.py:27
  1.0 3.4 %collective-permute-start = (bf16[3,4352]{1,0:T(4,128)(2,1)S(1)}, bf16[3,4352]{1,0:T(4,128)(2,1)S(1)}, u32[]{:S(2)}, u32[]{:S(2)}) collective-permute-start(bf16[3,4352]{1,0:T(4,128)(2,1)S(1)} %slice.37), channel_id=1, source_target_pairs={{0,2},{2,4},{4,6},{6,8},{8,10},{10,12},{12,14},{14,16},{16,18},{18... | collective-permute-start | bytes 78344 | tf_op jit(solution)/shard_map/ppermute | solution.py:21
  4.4 0.7 %exponential_negate_fusion = f32[64]{0:T(128)S(1)} fusion(f32[64]{0:T(128)} %param.15), kind=kLoop, calls=%fused_computation.50 | loop fusion | flops 64 | bytes 512 | tf_op jit(solution)/shard_map/neg | solution.py:261
  5.1 1.0 %fusion.11 = f32[128,64]{0,1:T(8,128)S(1)} fusion(f32[64]{0:T(128)S(1)} %exponential_negate_fusion, bf16[128,64]{0,1:T(8,128)(2,1)} %param.11, f32[64]{0:T(128)} %param.14), kind=kOutput, calls=%fused_computation.22 | convolution fusion | flops 12673024 | bytes 49664 | tf_op jit(solution)/shard_map/dot_general | solution.py:263
  6.1 0.1 slice.53
  6.2 0.1 copy.19
  6.2 0.8 %reduce-precision_convert_fusion = (bf16[128,64]{0,1:T(8,128)(2,1)S(1)}, bf16[128,64]{0,1:T(8,128)(2,1)S(1)}, f32[8,8,128]{2,1,0:T(8,128)S(1)}) fusion(f32[128,64]{0,1:T(8,128)S(1)} %fusion.11, f32[64]{0:T(128)S(1)} %bitcast.16, f32[64]{0:T(128)} %param.14, bf16[128,64]{0,1:T(8,128)(2,1)} %param.11), kind=kLoop, calls=%fused_computation.24 | loop fusion | flops 114688 | bytes 115200 | tf_op jit(solution)/shard_map/convert.7
  7.1 0.1 iota_compare_fusion
  7.3 0.3 convolution_convert_fusion.1
  7.6 0.0 copy-start.3
  7.6 1.2 %slice_reduce_fusion.3 = (f32[4352]{0:T(1024)S(1)}, f32[4352]{0:T(1024)S(1)}, f32[4352]{0:T(1024)S(1)}, f32[4352]{0:T(1024)S(1)}) fusion(f32[4,4352]{1,0:T(4,128)} %param.12), kind=kLoop, calls=%fused_computation.39 | loop fusion | bytes 139264 | tf_op jit(solution)/shard_map/slice | solution.py:31
  8.8 0.2 copy.18
  9.0 0.7 %broadcast_in_dim.4 = f32[64,64]{1,0:T(8,128)S(1)} broadcast(f32[64]{0:T(128)} %param.16), dimensions={0} | broadcast | bytes 16640 | tf_op jit(solution)/shard_map/broadcast_in_dim | solution.py:289
  9.8 0.1 broadcast_in_dim_reshape.3.skip
  9.9 0.0 collective-permute-done
  9.9 0.0 copy-done.2
  9.9 0.2 maximum_convert_fusion
  10.1 0.0 copy-done.3
  10.1 1.4 %multiply_convert_fusion.act = bf16[128,4352]{1,0:T(8,128)(2,1)S(1)} fusion(f32[131,4352]{1,0:T(8,128)S(1)} %maximum_convert_fusion, f32[4352]{0:T(1024)S(1)} %get-tuple-element.7, f32[4352]{0:T(1024)S(1)} %get-tuple-element.8, f32[4352]{0:T(1024)S(1)} %get-tuple-element.6, f32[4352]{0:T(1024)S(1)} %get-tuple-element.5, f32[4352]{0:T(1024)S(1)} %copy-done.3), kind=kLoop, calls=%fused_computation.12 | loop fusion | flops 7241728 | bytes 10114048 | tf_op jit(solution)/shard_map/convert_element_type | solution.py:32
  11.6 0.8 %convolution_convert_fusion = bf16[128,4096]{1,0:T(8,128)(2,1)S(1)} fusion(pred[64,4096]{1,0:T(32,128)(4,1)S(1)} %iota_compare_fusion, bf16[128,4352]{1,0:T(8,128)(2,1)S(1)} %multiply_convert_fusion.act, bf16[128,64]{0,1:T(8,128)(2,1)S(1)} %get-tuple-element.10, bf16[128,64]{0,1:T(8,128)(2,1)S(1)} %get-tuple-element.9), kind=kOutput, calls=%fused_computation.2 | convolution fusion | flops 271122432 | bytes 2424832 | tf_op jit(solution)/shard_map/dot_general | solution.py:274
  12.3 0.0 copy-start
  12.3 0.0 copy-start.1
  12.3 0.1 pad_maximum_fusion.s_ref
  12.5 31.0 %shard_map.91.entering = bf16[128,4096]{1,0:T(8,128)(2,1)S(1)} custom-call(bf16[144,4096]{1,0:T(8,128)(2,1)S(1)} %pad_maximum_fusion.s_ref), custom_call_target="tpu_custom_call" | custom-call | tf_op jit(solution)/shard_map/pallas_call | solution.py:176
  43.5 0.0 copy-done
  43.5 0.0 copy-done.1
  43.5 7.3 %shard_map.92 = bf16[128,4096]{1,0:T(8,128)(2,1)} custom-call(bf16[128,4352]{1,0:T(8,128)(2,1)S(1)} %multiply_convert_fusion.act, bf16[128,4096]{1,0:T(8,128)(2,1)S(1)} %shard_map.91.entering, bf16[128,4096]{1,0:T(8,128)(2,1)S(1)} %copy-done, f32[8,128,8]{2,1,0:T(8,128)S(1)} %bitcast.12, f32[8,8,128]{2,1,0:T(8,128)S(1)} %bitcast.14, ...), custom_call_target="tpu_custom_call" | custom-call | tf_op jit(solution)/shard_map/pallas_call | solution.py:290
  (6 shorter events, 0.1 us)
Async XLA Ops:
  0.0 9.9 %copy-start.2 = (bf16[128,4352]{1,0:T(8,128)(2,1)S(1)}, bf16[128,4352]{1,0:T(8,128)(2,1)}, u32[]{:S(2)}) copy-start(bf16[128,4352]{1,0:T(8,128)(2,1)} %param.9) | copy-start | bytes 3342340
  1.0 8.9 %collective-permute-start = (bf16[3,4352]{1,0:T(4,128)(2,1)S(1)}, bf16[3,4352]{1,0:T(4,128)(2,1)S(1)}, u32[]{:S(2)}, u32[]{:S(2)}) collective-permute-start(bf16[3,4352]{1,0:T(4,128)(2,1)S(1)} %slice.37), channel_id=1, source_target_pairs={{0,2},{2,4},{4,6},{6,8},{8,10},{10,12},{12,14},{14,16},{16,18},{18... | collective-permute-start | bytes 78344 | tf_op jit(solution)/shard_map/ppermute | solution.py:21
  7.6 2.6 %copy-start.3 = (f32[4352]{0:T(1024)S(1)}, f32[4352]{0:T(1024)}, u32[]{:S(2)}) copy-start(f32[4352]{0:T(1024)} %param.13) | copy-start | bytes 52228
  12.3 31.1 %copy-start = (bf16[128,4096]{1,0:T(8,128)(2,1)S(1)}, bf16[128,4096]{1,0:T(8,128)(2,1)}, u32[]{:S(2)}) copy-start(bf16[128,4096]{1,0:T(8,128)(2,1)} %gate.1) | copy-start | bytes 3145732
  12.3 31.1 %copy-start.1 = (f32[4096]{0:T(1024)S(1)}, f32[4096]{0:T(1024)}, u32[]{:S(2)}) copy-start(f32[4096]{0:T(1024)} %param.17) | copy-start | bytes 49156

commit v3 on v2

--- a/solution.py
+++ b/solution.py
@@ -32,8 +32,15 @@
     return jax.nn.silu(mixed).astype(jnp.bfloat16)
 
 
+def split(value):
+    high = value.astype(jnp.bfloat16)
+    low = (value - high.astype(jnp.float32)).astype(jnp.bfloat16)
+    return high, low
+
+
 def prefix_kernel(
-    count, group, s_ref, f_ref, got, ein, eout, fsend, gsum,
+    count, group, s_ref, act, gate, cols, rows_ref, steps, skip, gain,
+    out, f_ref, mixed, got, ein, eout, fsend, gsum,
     send_a, recv_a, send_c, recv_c, send_f, recv_f,
 ):
     rows = ein.shape[0]
@@ -104,6 +111,40 @@
             share(step, k).start()
     got[0] = s_ref[:, pl.ds(pl.multiple_of(mine * width, width), width)]
 
+    tokens = act.shape[0]
+    inner = f_ref.shape[1]
+    block = 8 * HEADDIM
+    blocks = inner // block
+    b_rows = act[:, inner : inner + STATE]
+    c_rows = act[:, inner + STATE : inner + 2 * STATE]
+    scores = lax.dot_general(c_rows, b_rows, (((1,), (1,)), ((), ())), preferred_element_type=jnp.float32)
+    lower = lax.broadcasted_iota(jnp.int32, (tokens, tokens), 0) >= lax.broadcasted_iota(jnp.int32, (tokens, tokens), 1)
+    scores = jnp.where(lower, scores, 0.0)
+    first = lax.broadcasted_iota(jnp.int32, (tokens, 2 * HEADDIM), 1) < HEADDIM
+
+    def inside_block(g, carry):
+        for pair in range(4):
+            columns = pl.ds(pl.multiple_of(g * block + pair * 128, 128), 128)
+            x = act[:, columns]
+            stacked = jnp.concatenate([x, x], axis=0)
+            halves = []
+            for half in range(2):
+                h = pair * 2 + half
+                col = cols[g, :, h : h + 1]
+                row = rows_ref[g, h : h + 1, :]
+                inside = jnp.exp(jnp.where(lower, col - row, -1e30)) * scores * steps[g, h : h + 1, :]
+                halves.append(
+                    jnp.dot(
+                        jnp.concatenate(split(inside), axis=1), stacked,
+                        preferred_element_type=jnp.float32,
+                    )
+                )
+            mixed[:, columns] = jnp.where(first, halves[0], halves[1]) + skip[:, columns] * x.astype(jnp.float32)
+        return carry
+
+    ahead = (blocks * plane) // max(planes - 1, 1)
+    lax.fori_loop(0, ahead, inside_block, 0)
+
     slots = [lax.rem(mine - i + group, group) for i in range(group)]
     for k in range(PARTS):
         columns = pl.ds(k * part, part)
@@ -146,6 +187,8 @@
         own = pl.ds(pl.multiple_of(mine * width + k * part, part), part)
         f_ref[:, own] = fsend[0, :, columns]
 
+    lax.fori_loop(ahead, blocks, inside_block, 0)
+
     for k in range(PARTS):
         for step in range(1, group):
             share(step, k).wait_send()
@@ -167,18 +210,42 @@
                 device_id_type=MESH,
             ).wait_recv()
 
-
-def entering_states(packed):
+    def outside_block(g, carry):
+        wide = pl.ds(pl.multiple_of(g * block, block), block)
+        outer = jnp.dot(c_rows, f_ref[:, wide], preferred_element_type=jnp.float32)
+        for pair in range(4):
+            columns = pl.ds(pl.multiple_of(g * block + pair * 128, 128), 128)
+            level = jnp.where(first, cols[g, :, 2 * pair : 2 * pair + 1], cols[g, :, 2 * pair + 1 : 2 * pair + 2])
+            mixed[:, columns] += jnp.exp(level) * outer[:, pair * 128 : pair * 128 + 128]
+        return carry
+
+    lax.fori_loop(0, blocks, outside_block, 0)
+
+    def norm(r, carry):
+        take = pl.ds(pl.multiple_of(r * 16, 16), 16)
+        z = gate[take, :].astype(jnp.float32)
+        result = mixed[take, :].astype(jnp.bfloat16).astype(jnp.float32)
+        gated = result * (z / (1.0 + jnp.exp(-z)))
+        spread = jnp.mean(gated * gated, axis=-1, keepdims=True)
+        out[take, :] = (gated * lax.rsqrt(spread + 1e-05) * gain[...]).astype(jnp.bfloat16)
+        return carry
+
+    lax.fori_loop(0, tokens // 16, norm, 0)
+
+
+def mixer(packed, activated, *others):
     count = lax.axis_size("seq")
     group = GROUP if count % GROUP == 0 else 1
     rows = packed.shape[0] - EXTRA
     width = packed.shape[1] // group
     return pl.pallas_call(
         functools.partial(prefix_kernel, count, group),
-        out_shape=jax.ShapeDtypeStruct((rows, packed.shape[1]), jnp.bfloat16),
-        in_specs=[pl.BlockSpec(memory_space=pltpu.VMEM)],
+        out_shape=jax.ShapeDtypeStruct((activated.shape[0], packed.shape[1]), jnp.bfloat16),
+        in_specs=[pl.BlockSpec(memory_space=pltpu.VMEM)] * (2 + len(others)),
         out_specs=pl.BlockSpec(memory_space=pltpu.VMEM),
         scratch_shapes=[
+            pltpu.VMEM((rows, packed.shape[1]), jnp.bfloat16),
+            pltpu.VMEM((activated.shape[0], packed.shape[1]), jnp.float32),
             pltpu.VMEM((group, rows + EXTRA, width), jnp.bfloat16),
             pltpu.VMEM((rows, width), jnp.bfloat16),
             pltpu.VMEM((rows, width), jnp.bfloat16),
@@ -194,59 +261,7 @@
         compiler_params=pltpu.CompilerParams(
             collective_id=0, has_side_effects=True, vmem_limit_bytes=32 * 1024 * 1024
         ),
-    )(packed)
-
-
-def split(value):
-    high = value.astype(jnp.bfloat16)
-    low = (value - high.astype(jnp.float32)).astype(jnp.bfloat16)
-    return high, low
-
-
-def mix_kernel(act, entering, gate, cols, rows_ref, steps, skip, gain, out, mixed):
-    tokens = act.shape[0]
-    inner = entering.shape[1]
-    block = 8 * HEADDIM
-    b_rows = act[:, inner : inner + STATE]
-    c_rows = act[:, inner + STATE : inner + 2 * STATE]
-    scores = lax.dot_general(c_rows, b_rows, (((1,), (1,)), ((), ())), preferred_element_type=jnp.float32)
-    lower = lax.broadcasted_iota(jnp.int32, (tokens, tokens), 0) >= lax.broadcasted_iota(jnp.int32, (tokens, tokens), 1)
-    scores = jnp.where(lower, scores, 0.0)
-    c_wide = c_rows.astype(jnp.float32)
-    first = lax.broadcasted_iota(jnp.int32, (tokens, 2 * HEADDIM), 1) < HEADDIM
-
-    def body(g, carry):
-        for pair in range(4):
-            columns = pl.ds(pl.multiple_of(g * block + pair * 128, 128), 128)
-            x = act[:, columns]
-            stacked = jnp.concatenate([x, entering[:, columns]], axis=0)
-            halves = []
-            for half in range(2):
-                h = pair * 2 + half
-                col = cols[g, :, h : h + 1]
-                row = rows_ref[g, h : h + 1, :]
-                inside = jnp.exp(jnp.where(lower, col - row, -1e30)) * scores * steps[g, h : h + 1, :]
-                whole = jnp.concatenate([inside, jnp.exp(col) * c_wide], axis=1)
-                high, low = split(whole)
-                halves.append(
-                    jnp.dot(high, stacked, preferred_element_type=jnp.float32)
-                    + jnp.dot(low, stacked, preferred_element_type=jnp.float32)
-                )
-            result = jnp.where(first, halves[0], halves[1]) + skip[:, columns] * x.astype(jnp.float32)
-            mixed[:, columns] = result.astype(jnp.bfloat16)
-        return carry
-
-    lax.fori_loop(0, inner // block, body, 0)
-
-    def norm(r, carry):
-        take = pl.ds(pl.multiple_of(r * 16, 16), 16)
-        z = gate[take, :].astype(jnp.float32)
-        gated = mixed[take, :].astype(jnp.float32) * (z / (1.0 + jnp.exp(-z)))
-        spread = jnp.mean(gated * gated, axis=-1, keepdims=True)
-        out[take, :] = (gated * lax.rsqrt(spread + 1e-05) * gain[...]).astype(jnp.bfloat16)
-        return carry
-
-    lax.fori_loop(0, tokens // 16, norm, 0)
+    )(packed, activated, *others)
 
 
 def shards(
@@ -281,20 +296,12 @@
     logs = jnp.stack([high, middle, low] + [jnp.zeros_like(low)] * (EXTRA - 3)).astype(jnp.bfloat16)
     logs = jnp.dot(logs, spread, preferred_element_type=jnp.float32).astype(jnp.bfloat16)
     packed = jnp.concatenate([state, logs], axis=0)
-    entering = entering_states(packed)
     groups = HEADS // 8
     cols = jnp.transpose(within.reshape(tokens, groups, 8), (1, 0, 2))
     rows = jnp.transpose(within).reshape(groups, 8, tokens)
     steps = jnp.transpose(step_size).reshape(groups, 8, tokens)
     skip = jnp.repeat(skip_gain, HEADDIM)[None, :]
-    return pl.pallas_call(
-        mix_kernel,
-        out_shape=jax.ShapeDtypeStruct((tokens, inner), jnp.bfloat16),
-        in_specs=[pl.BlockSpec(memory_space=pltpu.VMEM)] * 8,
-        out_specs=pl.BlockSpec(memory_space=pltpu.VMEM),
-        scratch_shapes=[pltpu.VMEM((tokens, inner), jnp.bfloat16)],
-        compiler_params=pltpu.CompilerParams(vmem_limit_bytes=32 * 1024 * 1024),
-    )(activated, entering, gate_input, cols, rows, steps, skip, norm_gain[None, :])
+    return mixer(packed, activated, gate_input, cols, rows, steps, skip, norm_gain[None, :])
 
 
 def solution(mesh):

time: 51.2 us -> 50.9 us (level)
  Pallas kernels: 38.3 us -> 34.9 us
  other arithmetic: 3.43 us -> 4.64 us
  matrix products: 2.01 us -> 2.98 us
  local copies, waits for them, and re-layouts: 3.48 us -> 4.45 us
    pallas_call x2 -> x1, Pallas kernels: 38.3 us -> 34.9 us  [mixer(): pl.pallas_call(functools.partial(prefix_kernel, count, group), out_shape=...]
    concatenate x1, other arithmetic: 0.1 us -> 1.32 us  [shards(): packed = jnp.concatenate([state, logs], axis=0)]
    dot_general x1, matrix products: 0.75 us -> 1.72 us  [shards(): lax.dot_general(activated[:, inner:inner + STATE], weighted, (((0,), (0,)...]
    unnamed x9 -> x10, local copies, waits for them, and re-layouts: 0.09 us -> 1.07 us
where the time goes in v3:
time: 50.9 us; the launch traced here: 50.5 us
  Pallas kernels  34.9 us (69%)
  other arithmetic  4.64 us (9%)
  local copies, waits for them, and re-layouts  4.45 us (9%)
  starting transfers between devices  3.4 us (7%)
  matrix products  2.98 us (6%)
    pallas_call x1, Pallas kernels, mixer(): pl.pallas_call(functools.partial(prefix_kernel, count, group), out_shape=...  34.9 us
    ppermute x1, starting transfers between devices, shifted(): lax.ppermute(value, axis, [(source, source + steps) for source in range(i...  3.4 us
    dot_general x1, matrix products, shards(): lax.dot_general(activated[:, inner:inner + STATE], weighted, (((0,), (0,)...  1.72 us
    convert_element_type x1, other arithmetic, convolve(): return jax.nn.silu(mixed).astype(jnp.bfloat16)  1.42 us
    concatenate x1, other arithmetic, shards(): packed = jnp.concatenate([state, logs], axis=0)  1.32 us
    slice x1, local copies, waits for them, and re-layouts, convolve(): conv_weight[offset][None, :] * padded[offset:offset + row_count]  1.25 us
    unnamed x10, local copies, waits for them, and re-layouts  1.07 us
  transfers between devices with their start and end apart: 1, of which 0 were waited for; matrix products, arithmetic and copies ran while one was open for 11% of the time, Pallas kernels for 0%

profile of v3, /device:TPU:24, one launch (start us, length us, event | category | flops | bytes accessed | tf_op | source)
XLA Modules:
  0.0 50.5 jit_solution(17501504310356117227)
XLA Ops:
  0.0 0.0 copy-start.2
  0.0 1.0 %slice.37 = bf16[3,4352]{1,0:T(4,128)(2,1)S(1)} slice(bf16[128,4352]{1,0:T(8,128)(2,1)} %param.9), slice={[125:128], [0:4352]} | slice | bytes 52224 | tf_op jit(solution)/shard_map/slice | solution.py:27
  1.0 3.4 %collective-permute-start = (bf16[3,4352]{1,0:T(4,128)(2,1)S(1)}, bf16[3,4352]{1,0:T(4,128)(2,1)S(1)}, u32[]{:S(2)}, u32[]{:S(2)}) collective-permute-start(bf16[3,4352]{1,0:T(4,128)(2,1)S(1)} %slice.37), channel_id=1, source_target_pairs={{0,2},{2,4},{4,6},{6,8},{8,10},{10,12},{12,14},{14,16},{16,18},{18... | collective-permute-start | bytes 78344 | tf_op jit(solution)/shard_map/ppermute | solution.py:21
  4.4 0.7 %exponential_negate_fusion = f32[64]{0:T(128)S(1)} fusion(f32[64]{0:T(128)} %param.15), kind=kLoop, calls=%fused_computation.50 | loop fusion | flops 64 | bytes 512 | tf_op jit(solution)/shard_map/neg | solution.py:276
  5.1 1.0 %fusion.11 = f32[128,64]{0,1:T(8,128)S(1)} fusion(f32[64]{0:T(128)S(1)} %exponential_negate_fusion, bf16[128,64]{0,1:T(8,128)(2,1)} %param.11, f32[64]{0:T(128)} %param.14), kind=kOutput, calls=%fused_computation.22 | convolution fusion | flops 12673024 | bytes 49664 | tf_op jit(solution)/shard_map/dot_general | solution.py:278
  6.1 0.1 slice.53
  6.2 0.1 copy.19
  6.2 0.8 %reduce-precision_convert_fusion = (bf16[128,64]{0,1:T(8,128)(2,1)S(1)}, bf16[128,64]{0,1:T(8,128)(2,1)S(1)}, f32[8,8,128]{2,1,0:T(8,128)S(1)}) fusion(f32[128,64]{0,1:T(8,128)S(1)} %fusion.11, f32[64]{0:T(128)S(1)} %bitcast.16, f32[64]{0:T(128)} %param.14, bf16[128,64]{0,1:T(8,128)(2,1)} %param.11), kind=kLoop, calls=%fused_computation.24 | loop fusion | flops 114688 | bytes 115200 | tf_op jit(solution)/shard_map/convert.7
  7.1 0.1 iota_compare_fusion
  7.3 0.3 convolution_convert_fusion.1
  7.6 0.0 copy-start.3
  7.6 1.2 %slice_reduce_fusion.3 = (f32[4352]{0:T(1024)S(1)}, f32[4352]{0:T(1024)S(1)}, f32[4352]{0:T(1024)S(1)}, f32[4352]{0:T(1024)S(1)}) fusion(f32[4,4352]{1,0:T(4,128)} %param.12), kind=kLoop, calls=%fused_computation.39 | loop fusion | bytes 139264 | tf_op jit(solution)/shard_map/slice | solution.py:31
  8.8 0.2 copy.18
  9.0 0.7 %broadcast_in_dim.4 = f32[64,64]{1,0:T(8,128)S(1)} broadcast(f32[64]{0:T(128)} %param.16), dimensions={0} | broadcast | bytes 16640 | tf_op jit(solution)/shard_map/broadcast_in_dim | solution.py:303
  9.8 0.1 broadcast_in_dim_reshape.3.skip
  9.9 0.0 collective-permute-done
  9.9 0.0 copy-done.2
  9.9 0.2 maximum_convert_fusion
  10.1 0.0 copy-done.3
  10.1 1.4 %multiply_convert_fusion.act = bf16[128,4352]{1,0:T(8,128)(2,1)S(1)} fusion(f32[131,4352]{1,0:T(8,128)S(1)} %maximum_convert_fusion, f32[4352]{0:T(1024)S(1)} %get-tuple-element.7, f32[4352]{0:T(1024)S(1)} %get-tuple-element.8, f32[4352]{0:T(1024)S(1)} %get-tuple-element.6, f32[4352]{0:T(1024)S(1)} %get-tuple-element.5, f32[4352]{0:T(1024)S(1)} %copy-done.3), kind=kLoop, calls=%fused_computation.12 | loop fusion | flops 7241728 | bytes 10114048 | tf_op jit(solution)/shard_map/convert_element_type | solution.py:32
  11.6 0.0 copy-start
  11.6 0.0 copy-start.1
  11.6 1.7 %convolution_convert_fusion = bf16[128,4096]{1,0:T(8,128)(2,1)} fusion(pred[64,4096]{1,0:T(32,128)(4,1)S(1)} %iota_compare_fusion, bf16[128,4352]{1,0:T(8,128)(2,1)S(1)} %multiply_convert_fusion.act, bf16[128,64]{0,1:T(8,128)(2,1)S(1)} %get-tuple-element.10, bf16[128,64]{0,1:T(8,128)(2,1)S(1)} %get-tuple-element.9), kind=kOutput, calls=%fused_computation.2 | convolution fusion | flops 271122432 | bytes 2424832 | tf_op jit(solution)/shard_map/dot_general | solution.py:289
  13.3 1.3 %pad_maximum_fusion.s_ref = bf16[144,4096]{1,0:T(8,128)(2,1)S(1)} fusion(bf16[16,4096]{1,0:T(8,128)(2,1)S(1)} %convolution_convert_fusion.1, bf16[128,4096]{1,0:T(8,128)(2,1)} %convolution_convert_fusion), kind=kLoop, calls=%fused_computation.17 | loop fusion | flops 2359296 | bytes 2359296 | tf_op jit(solution)/shard_map/concatenate | solution.py:298
  14.6 0.0 copy-done
  14.7 0.0 copy-done.1
  14.7 34.9 %shard_map.91 = bf16[128,4096]{1,0:T(8,128)(2,1)S(1)} custom-call(bf16[144,4096]{1,0:T(8,128)(2,1)S(1)} %pad_maximum_fusion.s_ref, bf16[128,4352]{1,0:T(8,128)(2,1)S(1)} %multiply_convert_fusion.act, bf16[128,4096]{1,0:T(8,128)(2,1)S(1)} %copy-done, f32[8,128,8]{2,1,0:T(8,128)S(1)} %bitcast.12, f32[8,8,128]{2,1,0:T(8,128)S(1)} %bitcast.14, ...), custom_call_target="tpu_custom_call" | custom-call | tf_op jit(solution)/shard_map/pallas_call | solution.py:241
  49.5 1.0 %copy.23 = bf16[128,4096]{1,0:T(8,128)(2,1)} copy(bf16[128,4096]{1,0:T(8,128)(2,1)S(1)} %shard_map.91) | data formatting | bytes 2097152
  (6 shorter events, 0.1 us)
Async XLA Ops:
  0.0 9.9 %copy-start.2 = (bf16[128,4352]{1,0:T(8,128)(2,1)S(1)}, bf16[128,4352]{1,0:T(8,128)(2,1)}, u32[]{:S(2)}) copy-start(bf16[128,4352]{1,0:T(8,128)(2,1)} %param.9) | copy-start | bytes 3342340
  1.0 8.9 %collective-permute-start = (bf16[3,4352]{1,0:T(4,128)(2,1)S(1)}, bf16[3,4352]{1,0:T(4,128)(2,1)S(1)}, u32[]{:S(2)}, u32[]{:S(2)}) collective-permute-start(bf16[3,4352]{1,0:T(4,128)(2,1)S(1)} %slice.37), channel_id=1, source_target_pairs={{0,2},{2,4},{4,6},{6,8},{8,10},{10,12},{12,14},{14,16},{16,18},{18... | collective-permute-start | bytes 78344 | tf_op jit(solution)/shard_map/ppermute | solution.py:21
  7.6 2.6 %copy-start.3 = (f32[4352]{0:T(1024)S(1)}, f32[4352]{0:T(1024)}, u32[]{:S(2)}) copy-start(f32[4352]{0:T(1024)} %param.13) | copy-start | bytes 52228
  11.6 3.1 %copy-start = (bf16[128,4096]{1,0:T(8,128)(2,1)S(1)}, bf16[128,4096]{1,0:T(8,128)(2,1)}, u32[]{:S(2)}) copy-start(bf16[128,4096]{1,0:T(8,128)(2,1)} %gate.1) | copy-start | bytes 3145732
  11.6 3.1 %copy-start.1 = (f32[4096]{0:T(1024)S(1)}, f32[4096]{0:T(1024)}, u32[]{:S(2)}) copy-start(f32[4096]{0:T(1024)} %param.17) | copy-start | bytes 49156

commit v4 on v3

--- a/solution.py
+++ b/solution.py
@@ -39,8 +39,8 @@
 
 
 def prefix_kernel(
-    count, group, s_ref, act, gate, cols, rows_ref, steps, skip, gain,
-    out, f_ref, mixed, got, ein, eout, fsend, gsum,
+    count, group, tails, logs, act, gate, cols, rows_ref, steps, skip, gain,
+    out, s_ref, f_ref, mixed, squares, got, ein, eout, fsend, gsum,
     send_a, recv_a, send_c, recv_c, send_f, recv_f,
 ):
     rows = ein.shape[0]
@@ -106,16 +106,37 @@
             device_id_type=MESH,
         )
 
-    for k in range(PARTS):
-        for step in range(1, group):
+    inner = f_ref.shape[1]
+    b_rows = act[:, inner : inner + STATE]
+    turned = jnp.transpose(b_rows.astype(jnp.float32)).astype(jnp.bfloat16)
+    factors = tails[...]
+    lane = lax.broadcasted_iota(jnp.int32, (2 * HEADS, part), 1)
+    head = lax.rem(lax.broadcasted_iota(jnp.int32, (2 * HEADS, part), 0), HEADS)
+
+    def local_state(start):
+        low = head * HEADDIM - start
+        spread = jnp.where((lane >= low) & (lane < low + HEADDIM), 1.0, 0.0).astype(jnp.bfloat16)
+        tail = jnp.dot(factors, spread, preferred_element_type=jnp.float32)
+        weighted = (tail * act[:, pl.ds(start, part)].astype(jnp.float32)).astype(jnp.bfloat16)
+        state = jnp.dot(turned, weighted, preferred_element_type=jnp.float32).astype(jnp.bfloat16)
+        return state, jnp.dot(logs[...], spread, preferred_element_type=jnp.float32).astype(jnp.bfloat16)
+
+    for k in range(PARTS):
+        for step in range(1, group):
+            member = lax.rem(mine + step, group)
+            start = pl.multiple_of(member * width + k * part, part)
+            state, marks = local_state(start)
+            s_ref[:rows, pl.ds(start, part)] = state
+            s_ref[rows:, pl.ds(start, part)] = marks
             share(step, k).start()
-    got[0] = s_ref[:, pl.ds(pl.multiple_of(mine * width, width), width)]
+    for k in range(PARTS):
+        state, marks = local_state(pl.multiple_of(mine * width + k * part, part))
+        got[0, :rows, pl.ds(k * part, part)] = state
+        got[0, rows:, pl.ds(k * part, part)] = marks
 
     tokens = act.shape[0]
-    inner = f_ref.shape[1]
     block = 8 * HEADDIM
     blocks = inner // block
-    b_rows = act[:, inner : inner + STATE]
     c_rows = act[:, inner + STATE : inner + 2 * STATE]
     scores = lax.dot_general(c_rows, b_rows, (((1,), (1,)), ((), ())), preferred_element_type=jnp.float32)
     lower = lax.broadcasted_iota(jnp.int32, (tokens, tokens), 0) >= lax.broadcasted_iota(jnp.int32, (tokens, tokens), 1)
@@ -189,16 +210,24 @@
 
     lax.fori_loop(ahead, blocks, inside_block, 0)
 
-    for k in range(PARTS):
-        for step in range(1, group):
-            share(step, k).wait_send()
-
-        @pl.when(has_next)
-        def _():
-            chain(k).wait_send()
-
-        for step in range(1, group):
-            back(step, k).wait_send()
+    def outside(source, k):
+        where = pl.multiple_of(source * width + k * part, part)
+        outer = jnp.dot(c_rows, f_ref[:, pl.ds(where, part)], preferred_element_type=jnp.float32)
+        for pair in range(part // 128):
+            offset = (k * part) // HEADDIM + 2 * pair
+            g, h = source * (width // block) + offset // 8, offset % 8
+            columns = pl.ds(pl.multiple_of(where + pair * 128, 128), 128)
+            level = jnp.where(first, cols[g, :, h : h + 1], cols[g, :, h + 1 : h + 2])
+            total = mixed[:, columns] + jnp.exp(level) * outer[:, pair * 128 : pair * 128 + 128]
+            z = gate[:, columns].astype(jnp.float32)
+            gated = total.astype(jnp.bfloat16).astype(jnp.float32) * (z / (1.0 + jnp.exp(-z)))
+            mixed[:, columns] = gated
+            squares[...] += gated * gated
+
+    squares[...] = jnp.zeros_like(squares)
+    for k in range(PARTS):
+        outside(mine, k)
+        for step in range(1, group):
             source = lax.rem(mine - step + group, group)
             landed = pl.ds(pl.multiple_of(source * width + k * part, part), part)
             pltpu.make_async_remote_copy(
@@ -209,43 +238,43 @@
                 device_id={"seq": base + lax.rem(mine + step, group)},
                 device_id_type=MESH,
             ).wait_recv()
-
-    def outside_block(g, carry):
-        wide = pl.ds(pl.multiple_of(g * block, block), block)
-        outer = jnp.dot(c_rows, f_ref[:, wide], preferred_element_type=jnp.float32)
-        for pair in range(4):
-            columns = pl.ds(pl.multiple_of(g * block + pair * 128, 128), 128)
-            level = jnp.where(first, cols[g, :, 2 * pair : 2 * pair + 1], cols[g, :, 2 * pair + 1 : 2 * pair + 2])
-            mixed[:, columns] += jnp.exp(level) * outer[:, pair * 128 : pair * 128 + 128]
-        return carry
-
-    lax.fori_loop(0, blocks, outside_block, 0)
+            outside(source, k)
 
     def norm(r, carry):
         take = pl.ds(pl.multiple_of(r * 16, 16), 16)
-        z = gate[take, :].astype(jnp.float32)
-        result = mixed[take, :].astype(jnp.bfloat16).astype(jnp.float32)
-        gated = result * (z / (1.0 + jnp.exp(-z)))
-        spread = jnp.mean(gated * gated, axis=-1, keepdims=True)
-        out[take, :] = (gated * lax.rsqrt(spread + 1e-05) * gain[...]).astype(jnp.bfloat16)
+        mean = jnp.sum(squares[take, :], axis=-1, keepdims=True) * (1.0 / inner)
+        out[take, :] = (mixed[take, :] * lax.rsqrt(mean + 1e-05) * gain[...]).astype(jnp.bfloat16)
         return carry
 
     lax.fori_loop(0, tokens // 16, norm, 0)
 
-
-def mixer(packed, activated, *others):
+    for k in range(PARTS):
+        for step in range(1, group):
+            share(step, k).wait_send()
+            back(step, k).wait_send()
+
+        @pl.when(has_next)
+        def _():
+            chain(k).wait_send()
+
+
+def mixer(tails, logs, activated, *others):
     count = lax.axis_size("seq")
     group = GROUP if count % GROUP == 0 else 1
-    rows = packed.shape[0] - EXTRA
-    width = packed.shape[1] // group
+    rows = STATE
+    inner = HEADS * HEADDIM
+    width = inner // group
+    tokens = activated.shape[0]
     return pl.pallas_call(
         functools.partial(prefix_kernel, count, group),
-        out_shape=jax.ShapeDtypeStruct((activated.shape[0], packed.shape[1]), jnp.bfloat16),
-        in_specs=[pl.BlockSpec(memory_space=pltpu.VMEM)] * (2 + len(others)),
+        out_shape=jax.ShapeDtypeStruct((tokens, inner), jnp.bfloat16),
+        in_specs=[pl.BlockSpec(memory_space=pltpu.VMEM)] * (3 + len(others)),
         out_specs=pl.BlockSpec(memory_space=pltpu.VMEM),
         scratch_shapes=[
-            pltpu.VMEM((rows, packed.shape[1]), jnp.bfloat16),
-            pltpu.VMEM((activated.shape[0], packed.shape[1]), jnp.float32),
+            pltpu.VMEM((rows + EXTRA, inner), jnp.bfloat16),
+            pltpu.VMEM((rows, inner), jnp.bfloat16),
+            pltpu.VMEM((tokens, inner), jnp.float32),
+            pltpu.VMEM((tokens, 128), jnp.float32),
             pltpu.VMEM((group, rows + EXTRA, width), jnp.bfloat16),
             pltpu.VMEM((rows, width), jnp.bfloat16),
             pltpu.VMEM((rows, width), jnp.bfloat16),
@@ -261,7 +290,7 @@
         compiler_params=pltpu.CompilerParams(
             collective_id=0, has_side_effects=True, vmem_limit_bytes=32 * 1024 * 1024
         ),
-    )(packed, activated, *others)
+    )(tails, logs, activated, *others)
 
 
 def shards(
@@ -277,31 +306,20 @@
     lower = (jnp.arange(tokens)[:, None] >= jnp.arange(tokens)[None, :]).astype(jnp.float32)
     within = jnp.dot(lower, step_size * rate[None, :], precision=highest)
     ends = within[-1]
-    spread = (jnp.arange(inner)[None, :] // HEADDIM == jnp.arange(HEADS)[:, None]).astype(jnp.bfloat16)
     tail = jnp.exp(ends[None, :] - within) * step_size
     top = lax.reduce_precision(tail, 8, 7)
-    tail = jnp.dot(
-        jnp.concatenate([top, tail - top], axis=1).astype(jnp.bfloat16),
-        jnp.concatenate([spread, spread], axis=0),
-        preferred_element_type=jnp.float32,
-    )
-    weighted = (tail * activated[:, :inner].astype(jnp.float32)).astype(jnp.bfloat16)
-    state = lax.dot_general(
-        activated[:, inner : inner + STATE], weighted, (((0,), (0,)), ((), ())),
-        preferred_element_type=jnp.float32,
-    ).astype(jnp.bfloat16)
+    tails = jnp.concatenate([top, tail - top], axis=1).astype(jnp.bfloat16)
     high = lax.reduce_precision(ends, 8, 7)
     middle = lax.reduce_precision(ends - high, 8, 7)
     low = lax.reduce_precision(ends - high - middle, 8, 7)
     logs = jnp.stack([high, middle, low] + [jnp.zeros_like(low)] * (EXTRA - 3)).astype(jnp.bfloat16)
-    logs = jnp.dot(logs, spread, preferred_element_type=jnp.float32).astype(jnp.bfloat16)
-    packed = jnp.concatenate([state, logs], axis=0)
+    logs = jnp.concatenate([logs, jnp.zeros_like(logs)], axis=1)
     groups = HEADS // 8
     cols = jnp.transpose(within.reshape(tokens, groups, 8), (1, 0, 2))
     rows = jnp.transpose(within).reshape(groups, 8, tokens)
     steps = jnp.transpose(step_size).reshape(groups, 8, tokens)
     skip = jnp.repeat(skip_gain, HEADDIM)[None, :]
-    return mixer(packed, activated, gate_input, cols, rows, steps, skip, norm_gain[None, :])
+    return mixer(tails, logs, activated, gate_input, cols, rows, steps, skip, norm_gain[None, :])
 
 
 def solution(mesh):

time: 50.9 us -> 46.1 us (0.906)
  matrix products: 2.98 us -> 0.91 us
  Pallas kernels: 34.9 us -> 32.9 us
  other arithmetic: 4.64 us -> 3.15 us
  local copies, waits for them, and re-layouts: 4.45 us -> 5.3 us
    pallas_call x1, Pallas kernels: 34.9 us -> 32.9 us  [mixer(): pl.pallas_call(functools.partial(prefix_kernel, count, group), out_shape=...]
    dot_general x2 -> x0, matrix products: 1.99 us -> none  [the longest x1 1.72 us: shards(): lax.dot_general(activated[:, inner:inner + STATE], weighted, (((0,), (0,)...]
    concatenate x1, other arithmetic: 1.32 us -> 0.09 us  [shards(): tails = jnp.concatenate([top, tail - top], axis=1).astype(jnp.bfloat16)]
    unnamed x10, local copies, waits for them, and re-layouts: 1.07 us -> 1.82 us
  transfers between devices with their start and end apart: 1 -> 1, of which waited for: 0 -> 0; matrix products, arithmetic and copies ran while one was open for 11% -> 12% of each run, Pallas kernels for 0% -> 0%
where the time goes in v4:
time: 46.1 us; the launch traced here: 45.8 us
  Pallas kernels  32.9 us (71%)
  local copies, waits for them, and re-layouts  5.3 us (11%)
  starting transfers between devices  3.4 us (7%)
  other arithmetic  3.15 us (7%)
  matrix products  0.91 us (2%)
    pallas_call x1, Pallas kernels, mixer(): pl.pallas_call(functools.partial(prefix_kernel, count, group), out_shape=...  32.9 us
    ppermute x1, starting transfers between devices, shifted(): lax.ppermute(value, axis, [(source, source + steps) for source in range(i...  3.4 us
    unnamed x10, local copies, waits for them, and re-layouts  1.82 us
    convert_element_type x1, other arithmetic, convolve(): return jax.nn.silu(mixed).astype(jnp.bfloat16)  1.42 us
    slice x1, local copies, waits for them, and re-layouts, convolve(): conv_weight[offset][None, :] * padded[offset:offset + row_count]  1.24 us
    slice x1, local copies, waits for them, and re-layouts, convolve(): earlier = shifted(conv_input[row_count - (tap_count - 1):], 'seq', 1)  1 us
  transfers between devices with their start and end apart: 1, of which 0 were waited for; matrix products, arithmetic and copies ran while one was open for 12% of the time, Pallas kernels for 0%

profile of v4, /device:TPU:24, one launch (start us, length us, event | category | flops | bytes accessed | tf_op | source)
XLA Modules:
  0.0 45.8 jit_solution(387760398503856965)
XLA Ops:
  0.0 0.0 copy-start.2
  0.0 1.0 %slice.32 = bf16[3,4352]{1,0:T(4,128)(2,1)S(1)} slice(bf16[128,4352]{1,0:T(8,128)(2,1)} %param.9), slice={[125:128], [0:4352]} | slice | bytes 52224 | tf_op jit(solution)/shard_map/slice | solution.py:27
  1.0 3.4 %collective-permute-start = (bf16[3,4352]{1,0:T(4,128)(2,1)S(1)}, bf16[3,4352]{1,0:T(4,128)(2,1)S(1)}, u32[]{:S(2)}, u32[]{:S(2)}) collective-permute-start(bf16[3,4352]{1,0:T(4,128)(2,1)S(1)} %slice.32), channel_id=1, source_target_pairs={{0,2},{2,4},{4,6},{6,8},{8,10},{10,12},{12,14},{14,16},{16,18},{18... | collective-permute-start | bytes 78344 | tf_op jit(solution)/shard_map/ppermute | solution.py:21
  4.4 0.8 %copy.19 = bf16[128,64]{1,0:T(8,128)(2,1)S(1)} copy(bf16[128,64]{0,1:T(8,128)(2,1)} %param.11) | data formatting | bytes 32768 | tf_op args[2]
  5.2 0.7 %exponential_negate_fusion = f32[64]{0:T(128)S(1)} fusion(f32[64]{0:T(128)} %param.15), kind=kLoop, calls=%fused_computation.31 | loop fusion | flops 64 | bytes 512 | tf_op jit(solution)/shard_map/neg | solution.py:305
  5.9 0.9 %fusion.5 = f32[128,64]{0,1:T(8,128)S(1)} fusion(f32[64]{0:T(128)S(1)} %exponential_negate_fusion, bf16[128,64]{1,0:T(8,128)(2,1)S(1)} %copy.19, f32[64]{0:T(128)} %param.14), kind=kOutput, calls=%fused_computation.15 | convolution fusion | flops 12673024 | bytes 49664 | tf_op jit(solution)/shard_map/dot_general | solution.py:307
  6.8 0.1 copy.20
  6.9 0.7 %reduce-precision_convert_fusion = (bf16[128,64]{1,0:T(8,128)(2,1)S(1)}, bf16[128,64]{1,0:T(8,128)(2,1)S(1)}, f32[64,128]{0,1:T(8,128)S(1)}) fusion(f32[64]{0:T(128)} %param.14, bf16[128,64]{1,0:T(8,128)(2,1)S(1)} %copy.19, f32[128,64]{1,0:T(8,128)S(1)} %copy.20, f32[64]{0:T(128)S(1)} %get-tuple-element.14), kind=kLoop, calls=%fused_computation.12 | loop fusion | flops 114688 | bytes 115200 | tf_op jit(solution)/shard_map/convert.6
  7.7 1.2 %slice_reduce_fusion.3 = (f32[4352]{0:T(1024)S(1)}, f32[4352]{0:T(1024)S(1)}, f32[4352]{0:T(1024)S(1)}, f32[4352]{0:T(1024)S(1)}) fusion(f32[4,4352]{1,0:T(4,128)} %param.12), kind=kLoop, calls=%fused_computation.24 | loop fusion | bytes 139264 | tf_op jit(solution)/shard_map/slice | solution.py:31
  8.9 0.0 copy-start.3
  8.9 0.1 pad_maximum_fusion.tails
  9.1 0.1 copy.24
  9.2 0.2 copy.23
  9.4 0.7 %broadcast_in_dim.4 = f32[64,64]{1,0:T(8,128)S(1)} broadcast(f32[64]{0:T(128)} %param.16), dimensions={0} | broadcast | bytes 16640 | tf_op jit(solution)/shard_map/broadcast_in_dim | solution.py:321
  10.1 0.1 broadcast_in_dim_reshape.3.skip
  10.2 0.0 collective-permute-done
  10.2 0.0 copy-done.2
  10.2 0.2 maximum_convert_fusion
  10.5 0.0 copy-done.3
  10.5 0.0 copy-start
  10.5 0.0 copy-start.1
  10.5 1.4 %multiply_convert_fusion.act = bf16[128,4352]{1,0:T(8,128)(2,1)S(1)} fusion(f32[131,4352]{1,0:T(8,128)S(1)} %maximum_convert_fusion, f32[4352]{0:T(1024)S(1)} %get-tuple-element.7, f32[4352]{0:T(1024)S(1)} %get-tuple-element.8, f32[4352]{0:T(1024)S(1)} %get-tuple-element.6, f32[4352]{0:T(1024)S(1)} %get-tuple-element.5, f32[4352]{0:T(1024)S(1)} %copy-done.3), kind=kLoop, calls=%fused_computation.8 | loop fusion | flops 7241728 | bytes 10114048 | tf_op jit(solution)/shard_map/convert_element_type | solution.py:32
  11.9 0.0 copy-done
  11.9 0.0 copy-done.1
  11.9 32.9 %shard_map.91 = bf16[128,4096]{1,0:T(8,128)(2,1)S(1)} custom-call(bf16[128,128]{1,0:T(8,128)(2,1)S(1)} %pad_maximum_fusion.tails, bf16[16,128]{1,0:T(8,128)(2,1)S(1)} %concatenate.11.logs, bf16[128,4352]{1,0:T(8,128)(2,1)S(1)} %multiply_convert_fusion.act, bf16[128,4096]{1,0:T(8,128)(2,1)S(1)} %copy-done, f32[8,128,8]{2,1,0:T(8,128)S(1)} %bitcast.11, ...), custom_call_target="tpu_custom_call" | custom-call | tf_op jit(solution)/shard_map/pallas_call | solution.py:268
  44.8 1.0 %copy.26 = bf16[128,4096]{1,0:T(8,128)(2,1)} copy(bf16[128,4096]{1,0:T(8,128)(2,1)S(1)} %shard_map.91) | data formatting | bytes 2097152
  (6 shorter events, 0.1 us)
Async XLA Ops:
  0.0 10.2 %copy-start.2 = (bf16[128,4352]{1,0:T(8,128)(2,1)S(1)}, bf16[128,4352]{1,0:T(8,128)(2,1)}, u32[]{:S(2)}) copy-start(bf16[128,4352]{1,0:T(8,128)(2,1)} %param.9) | copy-start | bytes 3342340
  1.0 9.2 %collective-permute-start = (bf16[3,4352]{1,0:T(4,128)(2,1)S(1)}, bf16[3,4352]{1,0:T(4,128)(2,1)S(1)}, u32[]{:S(2)}, u32[]{:S(2)}) collective-permute-start(bf16[3,4352]{1,0:T(4,128)(2,1)S(1)} %slice.32), channel_id=1, source_target_pairs={{0,2},{2,4},{4,6},{6,8},{8,10},{10,12},{12,14},{14,16},{16,18},{18... | collective-permute-start | bytes 78344 | tf_op jit(solution)/shard_map/ppermute | solution.py:21
  8.9 1.6 %copy-start.3 = (f32[4352]{0:T(1024)S(1)}, f32[4352]{0:T(1024)}, u32[]{:S(2)}) copy-start(f32[4352]{0:T(1024)} %param.13) | copy-start | bytes 52228
  10.5 1.4 %copy-start = (bf16[128,4096]{1,0:T(8,128)(2,1)S(1)}, bf16[128,4096]{1,0:T(8,128)(2,1)}, u32[]{:S(2)}) copy-start(bf16[128,4096]{1,0:T(8,128)(2,1)} %gate.1) | copy-start | bytes 3145732
  10.5 1.4 %copy-start.1 = (f32[4096]{0:T(1024)S(1)}, f32[4096]{0:T(1024)}, u32[]{:S(2)}) copy-start(f32[4096]{0:T(1024)} %param.17) | copy-start | bytes 49156

commit v5 on v4

--- a/solution.py
+++ b/solution.py
@@ -15,23 +15,6 @@
 MESH = pl.DeviceIdType.MESH
 
 
-def shifted(value, axis, steps):
-    count = lax.axis_size(axis)
-    initial, last = (max(0, -steps), min(count, count - steps))
-    return lax.ppermute(value, axis, [(source, source + steps) for source in range(initial, last)])
-
-
-def convolve(conv_input, conv_weight, convolution_bias):
-    tap_count = conv_weight.shape[0]
-    row_count = conv_input.shape[0]
-    earlier = shifted(conv_input[row_count - (tap_count - 1) :], "seq", 1)
-    padded = jnp.concatenate([earlier, conv_input], axis=0).astype(jnp.float32)
-    mixed = convolution_bias[None, :]
-    for offset in range(tap_count):
-        mixed = mixed + conv_weight[offset][None, :] * padded[offset : offset + row_count]
-    return jax.nn.silu(mixed).astype(jnp.bfloat16)
-
-
 def split(value):
     high = value.astype(jnp.bfloat16)
     low = (value - high.astype(jnp.float32)).astype(jnp.bfloat16)
@@ -39,9 +22,9 @@
 
 
 def prefix_kernel(
-    count, group, tails, logs, act, gate, cols, rows_ref, steps, skip, gain,
-    out, s_ref, f_ref, mixed, squares, got, ein, eout, fsend, gsum,
-    send_a, recv_a, send_c, recv_c, send_f, recv_f,
+    count, group, tails, logs, conv, weight, bias, gate, cols, rows_ref, steps, gain,
+    out, act, padded, halo, skip, s_ref, f_ref, mixed, squares, got, ein, eout, fsend, gsum,
+    send_h, recv_h, send_a, recv_a, send_c, recv_c, send_f, recv_f,
 ):
     rows = ein.shape[0]
     width = ein.shape[1]
@@ -69,7 +52,18 @@
     def _():
         pl.semaphore_signal(barrier, inc=1, device_id={"seq": after}, device_id_type=MESH)
 
-    peers = group - 1 + jnp.minimum(plane, 1) + jnp.minimum(planes - 1 - plane, 1)
+    is_last = mine // max(group - 1, 1)
+    is_first = 1 - jnp.minimum(mine, 1)
+
+    @pl.when(has_prev & (is_first == 1))
+    def _():
+        pl.semaphore_signal(barrier, inc=1, device_id={"seq": jnp.maximum(me - 1, 0)}, device_id_type=MESH)
+
+    @pl.when(has_next & (is_last == 1))
+    def _():
+        pl.semaphore_signal(barrier, inc=1, device_id={"seq": jnp.minimum(me + 1, count - 1)}, device_id_type=MESH)
+
+    peers = group - 1 + jnp.minimum(plane, 1) * (1 + is_first) + jnp.minimum(planes - 1 - plane, 1) * (1 + is_last)
     pl.semaphore_wait(barrier, peers)
 
     def share(step, k):
@@ -107,6 +101,41 @@
         )
 
     inner = f_ref.shape[1]
+    tokens = conv.shape[0]
+    taps = weight.shape[0]
+    hand_on = pltpu.make_async_remote_copy(
+        src_ref=conv.at[pl.ds(tokens - EXTRA, EXTRA)],
+        dst_ref=halo,
+        send_sem=send_h,
+        recv_sem=recv_h,
+        device_id={"seq": jnp.minimum(me + 1, count - 1)},
+        device_id_type=MESH,
+    )
+
+    @pl.when(me < count - 1)
+    def _():
+        hand_on.start()
+
+    padded[8:, :] = conv[...].astype(jnp.float32)
+
+    @pl.when(me == 0)
+    def _():
+        halo[...] = jnp.zeros_like(halo)
+
+    @pl.when(me > 0)
+    def _():
+        hand_on.wait_recv()
+
+    padded[:8, :] = halo[...].astype(jnp.float32)[8:]
+
+    def activate(start, size):
+        where = pl.ds(start, size)
+        value = bias[:, where]
+        for tap in range(taps):
+            value = value + weight[tap : tap + 1, where] * padded[pl.ds(9 - taps + tap, tokens), where]
+        act[:, where] = (value / (1.0 + jnp.exp(-value))).astype(jnp.bfloat16)
+
+    activate(inner, 2 * STATE)
     b_rows = act[:, inner : inner + STATE]
     turned = jnp.transpose(b_rows.astype(jnp.float32)).astype(jnp.bfloat16)
     factors = tails[...]
@@ -114,12 +143,15 @@
     head = lax.rem(lax.broadcasted_iota(jnp.int32, (2 * HEADS, part), 0), HEADS)
 
     def local_state(start):
+        activate(start, part)
         low = head * HEADDIM - start
         spread = jnp.where((lane >= low) & (lane < low + HEADDIM), 1.0, 0.0).astype(jnp.bfloat16)
         tail = jnp.dot(factors, spread, preferred_element_type=jnp.float32)
         weighted = (tail * act[:, pl.ds(start, part)].astype(jnp.float32)).astype(jnp.bfloat16)
         state = jnp.dot(turned, weighted, preferred_element_type=jnp.float32).astype(jnp.bfloat16)
-        return state, jnp.dot(logs[...], spread, preferred_element_type=jnp.float32).astype(jnp.bfloat16)
+        marks = jnp.dot(logs[...], spread, preferred_element_type=jnp.float32)
+        skip[0:1, pl.ds(start, part)] = marks[3:4] + marks[4:5] + marks[5:6]
+        return state, marks.astype(jnp.bfloat16)
 
     for k in range(PARTS):
         for step in range(1, group):
@@ -134,7 +166,6 @@
         got[0, :rows, pl.ds(k * part, part)] = state
         got[0, rows:, pl.ds(k * part, part)] = marks
 
-    tokens = act.shape[0]
     block = 8 * HEADDIM
     blocks = inner // block
     c_rows = act[:, inner + STATE : inner + 2 * STATE]
@@ -160,7 +191,7 @@
                         preferred_element_type=jnp.float32,
                     )
                 )
-            mixed[:, columns] = jnp.where(first, halves[0], halves[1]) + skip[:, columns] * x.astype(jnp.float32)
+            mixed[:, columns] = jnp.where(first, halves[0], halves[1]) + skip[0:1, columns] * x.astype(jnp.float32)
         return carry
 
     ahead = (blocks * plane) // max(planes - 1, 1)
@@ -248,6 +279,10 @@
 
     lax.fori_loop(0, tokens // 16, norm, 0)
 
+    @pl.when(me < count - 1)
+    def _():
+        hand_on.wait_send()
+
     for k in range(PARTS):
         for step in range(1, group):
             share(step, k).wait_send()
@@ -258,19 +293,23 @@
             chain(k).wait_send()
 
 
-def mixer(tails, logs, activated, *others):
+def mixer(tails, logs, conv_input, *others):
     count = lax.axis_size("seq")
     group = GROUP if count % GROUP == 0 else 1
     rows = STATE
     inner = HEADS * HEADDIM
     width = inner // group
-    tokens = activated.shape[0]
+    tokens = conv_input.shape[0]
     return pl.pallas_call(
         functools.partial(prefix_kernel, count, group),
         out_shape=jax.ShapeDtypeStruct((tokens, inner), jnp.bfloat16),
         in_specs=[pl.BlockSpec(memory_space=pltpu.VMEM)] * (3 + len(others)),
         out_specs=pl.BlockSpec(memory_space=pltpu.VMEM),
         scratch_shapes=[
+            pltpu.VMEM(conv_input.shape, jnp.bfloat16),
+            pltpu.VMEM((tokens + 8, conv_input.shape[1]), jnp.float32),
+            pltpu.VMEM((EXTRA, conv_input.shape[1]), jnp.bfloat16),
+            pltpu.VMEM((8, inner), jnp.float32),
             pltpu.VMEM((rows + EXTRA, inner), jnp.bfloat16),
             pltpu.VMEM((rows, inner), jnp.bfloat16),
             pltpu.VMEM((tokens, inner), jnp.float32),
@@ -280,6 +319,8 @@
             pltpu.VMEM((rows, width), jnp.bfloat16),
             pltpu.VMEM((group, rows, width), jnp.bfloat16),
             pltpu.VMEM((group, rows, width), jnp.float32),
+            pltpu.SemaphoreType.DMA,
+            pltpu.SemaphoreType.DMA,
             pltpu.SemaphoreType.DMA((group, PARTS)),
             pltpu.SemaphoreType.DMA((group, PARTS)),
             pltpu.SemaphoreType.DMA((PARTS,)),
@@ -288,9 +329,9 @@
             pltpu.SemaphoreType.DMA((group, PARTS)),
         ],
         compiler_params=pltpu.CompilerParams(
-            collective_id=0, has_side_effects=True, vmem_limit_bytes=32 * 1024 * 1024
+            collective_id=0, has_side_effects=True, vmem_limit_bytes=40 * 1024 * 1024
         ),
-    )(tails, logs, activated, *others)
+    )(tails, logs, conv_input, *others)
 
 
 def shards(
@@ -298,9 +339,7 @@
     step_bias, decay_log, skip_gain, norm_gain,
 ):
     highest = lax.Precision.HIGHEST
-    inner = HEADS * HEADDIM
     tokens = conv_input.shape[0]
-    activated = convolve(conv_input, conv_weight, convolution_bias)
     step_size = jax.nn.softplus(step_input.astype(jnp.float32) + step_bias[None, :])
     rate = -jnp.exp(decay_log)
     lower = (jnp.arange(tokens)[:, None] >= jnp.arange(tokens)[None, :]).astype(jnp.float32)
@@ -309,17 +348,21 @@
     tail = jnp.exp(ends[None, :] - within) * step_size
     top = lax.reduce_precision(tail, 8, 7)
     tails = jnp.concatenate([top, tail - top], axis=1).astype(jnp.bfloat16)
-    high = lax.reduce_precision(ends, 8, 7)
-    middle = lax.reduce_precision(ends - high, 8, 7)
-    low = lax.reduce_precision(ends - high - middle, 8, 7)
-    logs = jnp.stack([high, middle, low] + [jnp.zeros_like(low)] * (EXTRA - 3)).astype(jnp.bfloat16)
+    both = jnp.stack([ends, skip_gain])
+    high = lax.reduce_precision(both, 8, 7)
+    middle = lax.reduce_precision(both - high, 8, 7)
+    low = lax.reduce_precision(both - high - middle, 8, 7)
+    logs = jnp.transpose(jnp.stack([high, middle, low]), (1, 0, 2)).reshape(6, HEADS)
+    logs = jnp.pad(logs, ((0, EXTRA - 6), (0, 0))).astype(jnp.bfloat16)
     logs = jnp.concatenate([logs, jnp.zeros_like(logs)], axis=1)
     groups = HEADS // 8
     cols = jnp.transpose(within.reshape(tokens, groups, 8), (1, 0, 2))
     rows = jnp.transpose(within).reshape(groups, 8, tokens)
     steps = jnp.transpose(step_size).reshape(groups, 8, tokens)
-    skip = jnp.repeat(skip_gain, HEADDIM)[None, :]
-    return mixer(tails, logs, activated, gate_input, cols, rows, steps, skip, norm_gain[None, :])
+    return mixer(
+        tails, logs, conv_input, conv_weight, convolution_bias[None, :], gate_input,
+        cols, rows, steps, norm_gain[None, :],
+    )
 
 
 def solution(mesh):

time: 46.1 us -> 46.7 us (1.013)
  Pallas kernels: 32.9 us -> 38.8 us
  starting transfers between devices: 3.4 us -> 0 us
  local copies, waits for them, and re-layouts: 5.3 us -> 4.34 us
  other arithmetic: 3.15 us -> 2.26 us
    pallas_call x1, Pallas kernels: 32.9 us -> 38.8 us  [mixer(): pl.pallas_call(functools.partial(prefix_kernel, count, group), out_shape=...]
    ppermute x1 -> x0, starting transfers between devices: 3.4 us -> none  [shifted(): lax.ppermute(value, axis, [(source, source + steps) for source in range(i...]
    slice x2 -> x1, local copies, waits for them, and re-layouts: 2.23 us -> 0.17 us  [shards(): ends = within[-1]]
    convert_element_type x2 -> x0, other arithmetic: 1.66 us -> none  [the longest x1 1.42 us: convolve(): return jax.nn.silu(mixed).astype(jnp.bfloat16)]
    unnamed x10, local copies, waits for them, and re-layouts: 1.82 us -> 3.03 us
    another operation x2, other arithmetic: 0.74 us -> 1.4 us
  transfers between devices with their start and end apart: 1 -> 0, of which waited for: 0 -> 0; matrix products, arithmetic and copies ran while one was open for 12% -> 0% of each run, Pallas kernels for 0% -> 0%
where the time goes in v5:
time: 46.7 us; the launch traced here: 46.4 us
  Pallas kernels  38.8 us (83%)
  local copies, waits for them, and re-layouts  4.34 us (9%)
  other arithmetic  2.26 us (5%)
  matrix products  0.92 us (2%)
    pallas_call x1, Pallas kernels, mixer(): pl.pallas_call(functools.partial(prefix_kernel, count, group), out_shape=...  38.8 us
    unnamed x10, local copies, waits for them, and re-layouts  3.03 us
    another operation x2, other arithmetic  1.4 us

profile of v5, /device:TPU:24, one launch (start us, length us, event | category | flops | bytes accessed | tf_op | source)
XLA Modules:
  0.0 46.4 jit_solution(1998259414385734270)
XLA Ops:
  0.0 0.0 copy-start.3
  0.0 0.0 copy-start.2
  0.0 0.0 copy-start
  0.0 0.8 %exponential_negate_fusion = f32[64]{0:T(128)S(1)} fusion(f32[64]{0:T(128)} %param.15), kind=kLoop, calls=%fused_computation.20 | loop fusion | flops 64 | bytes 512 | tf_op jit(solution)/shard_map/neg | solution.py:344
  0.8 0.7 %broadcast_in_dim.4.bias = f32[1,4352]{1,0:T(1,128)S(1)} reshape(f32[4352]{0:T(1024)} %param.13) | data formatting | bytes 34816 | tf_op jit(solution)/shard_map/broadcast_in_dim | solution.py:363
  1.5 0.8 %copy.19 = bf16[128,64]{1,0:T(8,128)(2,1)S(1)} copy(bf16[128,64]{0,1:T(8,128)(2,1)} %param.11) | data formatting | bytes 32768 | tf_op args[2]
  2.3 0.9 %fusion.1 = f32[128,64]{0,1:T(8,128)S(1)} fusion(f32[64]{0:T(128)S(1)} %exponential_negate_fusion, bf16[128,64]{1,0:T(8,128)(2,1)S(1)} %copy.19, f32[64]{0:T(128)} %param.14), kind=kOutput, calls=%fused_computation.5 | convolution fusion | flops 12673024 | bytes 49664 | tf_op jit(solution)/shard_map/dot_general | solution.py:346
  3.3 0.2 slice_reduce_fusion
  3.4 0.7 %reduce-precision_convert_fusion.2 = (bf16[1,2,64]{2,1,0:T(2,128)(2,1)S(1)}, bf16[1,2,64]{2,1,0:T(2,128)(2,1)S(1)}, bf16[1,2,64]{2,1,0:T(2,128)(2,1)S(1)}) fusion(f32[1,1,64]{2,1,0:T(1,128)} %bitcast.19, f32[1,1,64]{2,1,0:T(1,128)S(1)} %bitcast.18), kind=kLoop, calls=%fused_computation.16 | loop fusion | flops 1152 | bytes 1280 | tf_op jit(solution)/shard_map/convert.4
  4.2 0.1 copy.21
  4.3 0.7 %reduce-precision_convert_fusion = (bf16[128,64]{1,0:T(8,128)(2,1)S(1)}, bf16[128,64]{1,0:T(8,128)(2,1)S(1)}, f32[64,128]{0,1:T(8,128)S(1)}) fusion(f32[64]{0:T(128)} %param.14, bf16[128,64]{1,0:T(8,128)(2,1)S(1)} %copy.19, f32[128,64]{1,0:T(8,128)S(1)} %copy.21, f32[64]{0:T(128)S(1)} %slice_reduce_fusion), kind=kLoop, calls=%fused_computation.2 | loop fusion | flops 114688 | bytes 115200 | tf_op jit(solution)/shard_map/convert.7
  5.0 0.1 pad_maximum_fusion.tails
  5.1 0.1 copy.24
  5.2 0.2 copy.23
  5.4 0.0 copy-done.3
  5.4 0.0 copy-done.2
  5.4 0.0 copy-done
  5.4 0.0 copy-start.1
  5.4 1.2 %copy-done.1 = bf16[128,4096]{1,0:T(8,128)(2,1)S(1)} copy-done((bf16[128,4096]{1,0:T(8,128)(2,1)S(1)}, bf16[128,4096]{1,0:T(8,128)(2,1)}, u32[]{:S(2)}) %copy-start.1) | copy-done | bytes 1048600
  6.6 38.8 %shard_map.91 = bf16[128,4096]{1,0:T(8,128)(2,1)S(1)} custom-call(bf16[128,128]{1,0:T(8,128)(2,1)S(1)} %pad_maximum_fusion.tails, bf16[16,128]{1,0:T(8,128)(2,1)S(1)} %pad.14.logs, bf16[128,4352]{1,0:T(8,128)(2,1)S(1)} %copy-done, f32[4,4352]{1,0:T(4,128)S(1)} %copy-done.2, f32[1,4352]{1,0:T(1,128)S(1)} %broadcast_in_dim.4.bias, ...), custom_call_target="tpu_custom_call" | custom-call | tf_op jit(solution)/shard_map/pallas_call | solution.py:303
  45.4 1.0 %copy.26 = bf16[128,4096]{1,0:T(8,128)(2,1)} copy(bf16[128,4096]{1,0:T(8,128)(2,1)S(1)} %shard_map.91) | data formatting | bytes 2097152
  (4 shorter events, 0.0 us)
Async XLA Ops:
  0.0 5.4 %copy-start.3 = (f32[4096]{0:T(1024)S(1)}, f32[4096]{0:T(1024)}, u32[]{:S(2)}) copy-start(f32[4096]{0:T(1024)} %param.17) | copy-start | bytes 49156
  0.0 5.4 %copy-start.2 = (f32[4,4352]{1,0:T(4,128)S(1)}, f32[4,4352]{1,0:T(4,128)}, u32[]{:S(2)}) copy-start(f32[4,4352]{1,0:T(4,128)} %weight.1) | copy-start | bytes 208900
  0.0 5.4 %copy-start = (bf16[128,4352]{1,0:T(8,128)(2,1)S(1)}, bf16[128,4352]{1,0:T(8,128)(2,1)}, u32[]{:S(2)}) copy-start(bf16[128,4352]{1,0:T(8,128)(2,1)} %conv.1) | copy-start | bytes 3342340
  5.4 1.2 %copy-start.1 = (bf16[128,4096]{1,0:T(8,128)(2,1)S(1)}, bf16[128,4096]{1,0:T(8,128)(2,1)}, u32[]{:S(2)}) copy-start(bf16[128,4096]{1,0:T(8,128)(2,1)} %gate.1) | copy-start | bytes 3145732

commit v6 on v4

--- a/solution.py
+++ b/solution.py
@@ -10,7 +10,7 @@
 STATE = 128
 HEADS = 64
 GROUP = 4
-PARTS = 4
+PARTS = 8
 EXTRA = 16
 MESH = pl.DeviceIdType.MESH
 

time: 46.1 us -> 45.5 us (0.987)
  Pallas kernels: 32.9 us -> 32 us
    pallas_call x1, Pallas kernels: 32.9 us -> 32 us  [mixer(): pl.pallas_call(functools.partial(prefix_kernel, count, group), out_shape=...]
  transfers between devices with their start and end apart: 1 -> 1, of which waited for: 0 -> 0; matrix products, arithmetic and copies ran while one was open for 12% -> 13% of each run, Pallas kernels for 0% -> 0%
where the time goes in v6:
time: 45.5 us; the launch traced here: 44.9 us
  Pallas kernels  32 us (70%)
  local copies, waits for them, and re-layouts  5.3 us (12%)
  starting transfers between devices  3.4 us (7%)
  other arithmetic  3.15 us (7%)
  matrix products  0.91 us (2%)
    pallas_call x1, Pallas kernels, mixer(): pl.pallas_call(functools.partial(prefix_kernel, count, group), out_shape=...  32 us
    ppermute x1, starting transfers between devices, shifted(): lax.ppermute(value, axis, [(source, source + steps) for source in range(i...  3.4 us
    unnamed x10, local copies, waits for them, and re-layouts  1.82 us
    convert_element_type x1, other arithmetic, convolve(): return jax.nn.silu(mixed).astype(jnp.bfloat16)  1.42 us
    slice x1, local copies, waits for them, and re-layouts, convolve(): conv_weight[offset][None, :] * padded[offset:offset + row_count]  1.24 us
    slice x1, local copies, waits for them, and re-layouts, convolve(): earlier = shifted(conv_input[row_count - (tap_count - 1):], 'seq', 1)  1 us
  transfers between devices with their start and end apart: 1, of which 0 were waited for; matrix products, arithmetic and copies ran while one was open for 13% of the time, Pallas kernels for 0%

profile of v6, /device:TPU:24, one launch (start us, length us, event | category | flops | bytes accessed | tf_op | source)
XLA Modules:
  0.0 44.9 jit_solution(5566706705952117387)
XLA Ops:
  0.0 0.0 copy-start.2
  0.0 1.0 %slice.32 = bf16[3,4352]{1,0:T(4,128)(2,1)S(1)} slice(bf16[128,4352]{1,0:T(8,128)(2,1)} %param.9), slice={[125:128], [0:4352]} | slice | bytes 52224 | tf_op jit(solution)/shard_map/slice | solution.py:27
  1.0 3.4 %collective-permute-start = (bf16[3,4352]{1,0:T(4,128)(2,1)S(1)}, bf16[3,4352]{1,0:T(4,128)(2,1)S(1)}, u32[]{:S(2)}, u32[]{:S(2)}) collective-permute-start(bf16[3,4352]{1,0:T(4,128)(2,1)S(1)} %slice.32), channel_id=1, source_target_pairs={{0,2},{2,4},{4,6},{6,8},{8,10},{10,12},{12,14},{14,16},{16,18},{18... | collective-permute-start | bytes 78344 | tf_op jit(solution)/shard_map/ppermute | solution.py:21
  4.4 0.8 %copy.19 = bf16[128,64]{1,0:T(8,128)(2,1)S(1)} copy(bf16[128,64]{0,1:T(8,128)(2,1)} %param.11) | data formatting | bytes 32768 | tf_op args[2]
  5.2 0.7 %exponential_negate_fusion = f32[64]{0:T(128)S(1)} fusion(f32[64]{0:T(128)} %param.15), kind=kLoop, calls=%fused_computation.31 | loop fusion | flops 64 | bytes 512 | tf_op jit(solution)/shard_map/neg | solution.py:305
  5.9 0.9 %fusion.5 = f32[128,64]{0,1:T(8,128)S(1)} fusion(f32[64]{0:T(128)S(1)} %exponential_negate_fusion, bf16[128,64]{1,0:T(8,128)(2,1)S(1)} %copy.19, f32[64]{0:T(128)} %param.14), kind=kOutput, calls=%fused_computation.15 | convolution fusion | flops 12673024 | bytes 49664 | tf_op jit(solution)/shard_map/dot_general | solution.py:307
  6.8 0.1 copy.20
  6.9 0.7 %reduce-precision_convert_fusion = (bf16[128,64]{1,0:T(8,128)(2,1)S(1)}, bf16[128,64]{1,0:T(8,128)(2,1)S(1)}, f32[64,128]{0,1:T(8,128)S(1)}) fusion(f32[64]{0:T(128)} %param.14, bf16[128,64]{1,0:T(8,128)(2,1)S(1)} %copy.19, f32[128,64]{1,0:T(8,128)S(1)} %copy.20, f32[64]{0:T(128)S(1)} %get-tuple-element.14), kind=kLoop, calls=%fused_computation.12 | loop fusion | flops 114688 | bytes 115200 | tf_op jit(solution)/shard_map/convert.6
  7.7 1.2 %slice_reduce_fusion.3 = (f32[4352]{0:T(1024)S(1)}, f32[4352]{0:T(1024)S(1)}, f32[4352]{0:T(1024)S(1)}, f32[4352]{0:T(1024)S(1)}) fusion(f32[4,4352]{1,0:T(4,128)} %param.12), kind=kLoop, calls=%fused_computation.24 | loop fusion | bytes 139264 | tf_op jit(solution)/shard_map/slice | solution.py:31
  8.9 0.0 copy-start.3
  8.9 0.1 pad_maximum_fusion.tails
  9.1 0.1 copy.24
  9.2 0.2 copy.23
  9.4 0.7 %broadcast_in_dim.4 = f32[64,64]{1,0:T(8,128)S(1)} broadcast(f32[64]{0:T(128)} %param.16), dimensions={0} | broadcast | bytes 16640 | tf_op jit(solution)/shard_map/broadcast_in_dim | solution.py:321
  10.1 0.1 broadcast_in_dim_reshape.3.skip
  10.2 0.0 collective-permute-done
  10.2 0.0 copy-done.2
  10.2 0.2 maximum_convert_fusion
  10.5 0.0 copy-done.3
  10.5 0.0 copy-start
  10.5 0.0 copy-start.1
  10.5 1.4 %multiply_convert_fusion.act = bf16[128,4352]{1,0:T(8,128)(2,1)S(1)} fusion(f32[131,4352]{1,0:T(8,128)S(1)} %maximum_convert_fusion, f32[4352]{0:T(1024)S(1)} %get-tuple-element.7, f32[4352]{0:T(1024)S(1)} %get-tuple-element.8, f32[4352]{0:T(1024)S(1)} %get-tuple-element.6, f32[4352]{0:T(1024)S(1)} %get-tuple-element.5, f32[4352]{0:T(1024)S(1)} %copy-done.3), kind=kLoop, calls=%fused_computation.8 | loop fusion | flops 7241728 | bytes 10114048 | tf_op jit(solution)/shard_map/convert_element_type | solution.py:32
  11.9 0.0 copy-done
  11.9 0.0 copy-done.1
  11.9 32.0 %shard_map.91 = bf16[128,4096]{1,0:T(8,128)(2,1)S(1)} custom-call(bf16[128,128]{1,0:T(8,128)(2,1)S(1)} %pad_maximum_fusion.tails, bf16[16,128]{1,0:T(8,128)(2,1)S(1)} %concatenate.11.logs, bf16[128,4352]{1,0:T(8,128)(2,1)S(1)} %multiply_convert_fusion.act, bf16[128,4096]{1,0:T(8,128)(2,1)S(1)} %copy-done, f32[8,128,8]{2,1,0:T(8,128)S(1)} %bitcast.11, ...), custom_call_target="tpu_custom_call" | custom-call | tf_op jit(solution)/shard_map/pallas_call | solution.py:268
  43.9 1.0 %copy.26 = bf16[128,4096]{1,0:T(8,128)(2,1)} copy(bf16[128,4096]{1,0:T(8,128)(2,1)S(1)} %shard_map.91) | data formatting | bytes 2097152
  (6 shorter events, 0.1 us)
Async XLA Ops:
  0.0 10.2 %copy-start.2 = (bf16[128,4352]{1,0:T(8,128)(2,1)S(1)}, bf16[128,4352]{1,0:T(8,128)(2,1)}, u32[]{:S(2)}) copy-start(bf16[128,4352]{1,0:T(8,128)(2,1)} %param.9) | copy-start | bytes 3342340
  1.0 9.2 %collective-permute-start = (bf16[3,4352]{1,0:T(4,128)(2,1)S(1)}, bf16[3,4352]{1,0:T(4,128)(2,1)S(1)}, u32[]{:S(2)}, u32[]{:S(2)}) collective-permute-start(bf16[3,4352]{1,0:T(4,128)(2,1)S(1)} %slice.32), channel_id=1, source_target_pairs={{0,2},{2,4},{4,6},{6,8},{8,10},{10,12},{12,14},{14,16},{16,18},{18... | collective-permute-start | bytes 78344 | tf_op jit(solution)/shard_map/ppermute | solution.py:21
  8.9 1.6 %copy-start.3 = (f32[4352]{0:T(1024)S(1)}, f32[4352]{0:T(1024)}, u32[]{:S(2)}) copy-start(f32[4352]{0:T(1024)} %param.13) | copy-start | bytes 52228
  10.5 1.4 %copy-start = (bf16[128,4096]{1,0:T(8,128)(2,1)S(1)}, bf16[128,4096]{1,0:T(8,128)(2,1)}, u32[]{:S(2)}) copy-start(bf16[128,4096]{1,0:T(8,128)(2,1)} %gate.1) | copy-start | bytes 3145732
  10.5 1.4 %copy-start.1 = (f32[4096]{0:T(1024)S(1)}, f32[4096]{0:T(1024)}, u32[]{:S(2)}) copy-start(f32[4096]{0:T(1024)} %param.17) | copy-start | bytes 49156

commit v7 on v6

--- a/solution.py
+++ b/solution.py
@@ -39,8 +39,8 @@
 
 
 def prefix_kernel(
-    count, group, tails, logs, act, gate, cols, rows_ref, steps, skip, gain,
-    out, s_ref, f_ref, mixed, squares, got, ein, eout, fsend, gsum,
+    count, group, tails, logs, act, gate, cols, rows_ref, steps, gain,
+    out, skip, s_ref, f_ref, mixed, squares, got, ein, eout, fsend, gsum,
     send_a, recv_a, send_c, recv_c, send_f, recv_f,
 ):
     rows = ein.shape[0]
@@ -119,7 +119,9 @@
         tail = jnp.dot(factors, spread, preferred_element_type=jnp.float32)
         weighted = (tail * act[:, pl.ds(start, part)].astype(jnp.float32)).astype(jnp.bfloat16)
         state = jnp.dot(turned, weighted, preferred_element_type=jnp.float32).astype(jnp.bfloat16)
-        return state, jnp.dot(logs[...], spread, preferred_element_type=jnp.float32).astype(jnp.bfloat16)
+        marks = jnp.dot(logs[...], spread, preferred_element_type=jnp.float32)
+        skip[0:1, pl.ds(start, part)] = marks[3:4] + marks[4:5] + marks[5:6]
+        return state, marks.astype(jnp.bfloat16)
 
     for k in range(PARTS):
         for step in range(1, group):
@@ -160,7 +162,7 @@
                         preferred_element_type=jnp.float32,
                     )
                 )
-            mixed[:, columns] = jnp.where(first, halves[0], halves[1]) + skip[:, columns] * x.astype(jnp.float32)
+            mixed[:, columns] = jnp.where(first, halves[0], halves[1]) + skip[0:1, columns] * x.astype(jnp.float32)
         return carry
 
     ahead = (blocks * plane) // max(planes - 1, 1)
@@ -271,6 +273,7 @@
         in_specs=[pl.BlockSpec(memory_space=pltpu.VMEM)] * (3 + len(others)),
         out_specs=pl.BlockSpec(memory_space=pltpu.VMEM),
         scratch_shapes=[
+            pltpu.VMEM((8, inner), jnp.float32),
             pltpu.VMEM((rows + EXTRA, inner), jnp.bfloat16),
             pltpu.VMEM((rows, inner), jnp.bfloat16),
             pltpu.VMEM((tokens, inner), jnp.float32),
@@ -309,17 +312,18 @@
     tail = jnp.exp(ends[None, :] - within) * step_size
     top = lax.reduce_precision(tail, 8, 7)
     tails = jnp.concatenate([top, tail - top], axis=1).astype(jnp.bfloat16)
-    high = lax.reduce_precision(ends, 8, 7)
-    middle = lax.reduce_precision(ends - high, 8, 7)
-    low = lax.reduce_precision(ends - high - middle, 8, 7)
-    logs = jnp.stack([high, middle, low] + [jnp.zeros_like(low)] * (EXTRA - 3)).astype(jnp.bfloat16)
+    both = jnp.stack([ends, skip_gain])
+    high = lax.reduce_precision(both, 8, 7)
+    middle = lax.reduce_precision(both - high, 8, 7)
+    low = lax.reduce_precision(both - high - middle, 8, 7)
+    logs = jnp.transpose(jnp.stack([high, middle, low]), (1, 0, 2)).reshape(6, HEADS)
+    logs = jnp.pad(logs, ((0, EXTRA - 6), (0, 0))).astype(jnp.bfloat16)
     logs = jnp.concatenate([logs, jnp.zeros_like(logs)], axis=1)
     groups = HEADS // 8
     cols = jnp.transpose(within.reshape(tokens, groups, 8), (1, 0, 2))
     rows = jnp.transpose(within).reshape(groups, 8, tokens)
     steps = jnp.transpose(step_size).reshape(groups, 8, tokens)
-    skip = jnp.repeat(skip_gain, HEADDIM)[None, :]
-    return mixer(tails, logs, activated, gate_input, cols, rows, steps, skip, norm_gain[None, :])
+    return mixer(tails, logs, activated, gate_input, cols, rows, steps, norm_gain[None, :])
 
 
 def solution(mesh):

time: 45.5 us -> 45.5 us (level)
  other arithmetic: 3.15 us -> 3.83 us
  local copies, waits for them, and re-layouts: 5.3 us -> 4.63 us
    broadcast_in_dim x1 -> x0, local copies, waits for them, and re-layouts: 0.73 us -> none  [shards(): skip = jnp.repeat(skip_gain, HEADDIM)[None, :]]
    another operation x2, other arithmetic: 0.74 us -> 1.4 us
where the time goes in v7:
time: 45.5 us; the launch traced here: 44.9 us
  Pallas kernels  32 us (70%)
  local copies, waits for them, and re-layouts  4.63 us (10%)
  other arithmetic  3.83 us (8%)
  starting transfers between devices  3.4 us (7%)
  matrix products  0.91 us (2%)
    pallas_call x1, Pallas kernels, mixer(): pl.pallas_call(functools.partial(prefix_kernel, count, group), out_shape=...  32 us
    ppermute x1, starting transfers between devices, shifted(): lax.ppermute(value, axis, [(source, source + steps) for source in range(i...  3.4 us
    unnamed x10, local copies, waits for them, and re-layouts  1.82 us
    convert_element_type x1, other arithmetic, convolve(): return jax.nn.silu(mixed).astype(jnp.bfloat16)  1.42 us
    another operation x2, other arithmetic  1.4 us
    slice x1, local copies, waits for them, and re-layouts, convolve(): conv_weight[offset][None, :] * padded[offset:offset + row_count]  1.24 us
    slice x1, local copies, waits for them, and re-layouts, convolve(): earlier = shifted(conv_input[row_count - (tap_count - 1):], 'seq', 1)  1 us
  transfers between devices with their start and end apart: 1, of which 0 were waited for; matrix products, arithmetic and copies ran while one was open for 13% of the time, Pallas kernels for 0%

profile of v7, /device:TPU:24, one launch (start us, length us, event | category | flops | bytes accessed | tf_op | source)
XLA Modules:
  0.0 44.9 jit_solution(9980989849695041242)
XLA Ops:
  0.0 0.0 copy-start.2
  0.0 1.0 %slice.32 = bf16[3,4352]{1,0:T(4,128)(2,1)S(1)} slice(bf16[128,4352]{1,0:T(8,128)(2,1)} %param.9), slice={[125:128], [0:4352]} | slice | bytes 52224 | tf_op jit(solution)/shard_map/slice | solution.py:27
  1.0 3.4 %collective-permute-start = (bf16[3,4352]{1,0:T(4,128)(2,1)S(1)}, bf16[3,4352]{1,0:T(4,128)(2,1)S(1)}, u32[]{:S(2)}, u32[]{:S(2)}) collective-permute-start(bf16[3,4352]{1,0:T(4,128)(2,1)S(1)} %slice.32), channel_id=1, source_target_pairs={{0,2},{2,4},{4,6},{6,8},{8,10},{10,12},{12,14},{14,16},{16,18},{18... | collective-permute-start | bytes 78344 | tf_op jit(solution)/shard_map/ppermute | solution.py:21
  4.4 0.8 %copy.19 = bf16[128,64]{1,0:T(8,128)(2,1)S(1)} copy(bf16[128,64]{0,1:T(8,128)(2,1)} %param.11) | data formatting | bytes 32768 | tf_op args[2]
  5.2 0.7 %exponential_negate_fusion = f32[64]{0:T(128)S(1)} fusion(f32[64]{0:T(128)} %param.15), kind=kLoop, calls=%fused_computation.34 | loop fusion | flops 64 | bytes 512 | tf_op jit(solution)/shard_map/neg | solution.py:308
  5.9 0.9 %fusion.5 = f32[128,64]{0,1:T(8,128)S(1)} fusion(f32[64]{0:T(128)S(1)} %exponential_negate_fusion, bf16[128,64]{1,0:T(8,128)(2,1)S(1)} %copy.19, f32[64]{0:T(128)} %param.14), kind=kOutput, calls=%fused_computation.15 | convolution fusion | flops 12673024 | bytes 49664 | tf_op jit(solution)/shard_map/dot_general | solution.py:310
  6.8 0.2 slice_reduce_fusion
  7.0 0.1 copy.21
  7.1 1.2 %slice_reduce_fusion.4 = (f32[4352]{0:T(1024)S(1)}, f32[4352]{0:T(1024)S(1)}, f32[4352]{0:T(1024)S(1)}, f32[4352]{0:T(1024)S(1)}) fusion(f32[4,4352]{1,0:T(4,128)} %param.12), kind=kLoop, calls=%fused_computation.25 | loop fusion | bytes 139264 | tf_op jit(solution)/shard_map/slice | solution.py:31
  8.3 0.0 copy-start.3
  8.4 0.7 %reduce-precision_convert_fusion = (bf16[128,64]{1,0:T(8,128)(2,1)S(1)}, bf16[128,64]{1,0:T(8,128)(2,1)S(1)}, f32[64,128]{0,1:T(8,128)S(1)}) fusion(f32[64]{0:T(128)} %param.14, bf16[128,64]{1,0:T(8,128)(2,1)S(1)} %copy.19, f32[128,64]{1,0:T(8,128)S(1)} %copy.21, f32[64]{0:T(128)S(1)} %slice_reduce_fusion), kind=kLoop, calls=%fused_computation.12 | loop fusion | flops 114688 | bytes 115200 | tf_op jit(solution)/shard_map/convert.7
  9.1 0.1 pad_maximum_fusion.tails
  9.2 0.7 %reduce-precision_convert_fusion.2 = (bf16[1,2,64]{2,1,0:T(2,128)(2,1)S(1)}, bf16[1,2,64]{2,1,0:T(2,128)(2,1)S(1)}, bf16[1,2,64]{2,1,0:T(2,128)(2,1)S(1)}) fusion(f32[1,1,64]{2,1,0:T(1,128)} %bitcast.19, f32[1,1,64]{2,1,0:T(1,128)S(1)} %bitcast.18), kind=kLoop, calls=%fused_computation.30 | loop fusion | flops 1152 | bytes 1280 | tf_op jit(solution)/shard_map/convert.4
  9.9 0.1 copy.24
  10.0 0.2 copy.23
  10.2 0.0 collective-permute-done
  10.2 0.0 copy-done.2
  10.2 0.2 maximum_convert_fusion
  10.5 0.0 copy-done.3
  10.5 0.0 copy-start
  10.5 0.0 copy-start.1
  10.5 1.4 %multiply_convert_fusion.act = bf16[128,4352]{1,0:T(8,128)(2,1)S(1)} fusion(f32[131,4352]{1,0:T(8,128)S(1)} %maximum_convert_fusion, f32[4352]{0:T(1024)S(1)} %get-tuple-element.7, f32[4352]{0:T(1024)S(1)} %get-tuple-element.8, f32[4352]{0:T(1024)S(1)} %get-tuple-element.6, f32[4352]{0:T(1024)S(1)} %get-tuple-element.5, f32[4352]{0:T(1024)S(1)} %copy-done.3), kind=kLoop, calls=%fused_computation.8 | loop fusion | flops 7241728 | bytes 10114048 | tf_op jit(solution)/shard_map/convert_element_type | solution.py:32
  11.9 0.0 copy-done
  11.9 0.0 copy-done.1
  11.9 32.0 %shard_map.91 = bf16[128,4096]{1,0:T(8,128)(2,1)S(1)} custom-call(bf16[128,128]{1,0:T(8,128)(2,1)S(1)} %pad_maximum_fusion.tails, bf16[16,128]{1,0:T(8,128)(2,1)S(1)} %pad.16.logs, bf16[128,4352]{1,0:T(8,128)(2,1)S(1)} %multiply_convert_fusion.act, bf16[128,4096]{1,0:T(8,128)(2,1)S(1)} %copy-done, f32[8,128,8]{2,1,0:T(8,128)S(1)} %bitcast.13, ...), custom_call_target="tpu_custom_call" | custom-call | tf_op jit(solution)/shard_map/pallas_call | solution.py:270
  43.9 1.0 %copy.26 = bf16[128,4096]{1,0:T(8,128)(2,1)} copy(bf16[128,4096]{1,0:T(8,128)(2,1)S(1)} %shard_map.91) | data formatting | bytes 2097152
  (4 shorter events, 0.0 us)
Async XLA Ops:
  0.0 10.2 %copy-start.2 = (bf16[128,4352]{1,0:T(8,128)(2,1)S(1)}, bf16[128,4352]{1,0:T(8,128)(2,1)}, u32[]{:S(2)}) copy-start(bf16[128,4352]{1,0:T(8,128)(2,1)} %param.9) | copy-start | bytes 3342340
  1.0 9.2 %collective-permute-start = (bf16[3,4352]{1,0:T(4,128)(2,1)S(1)}, bf16[3,4352]{1,0:T(4,128)(2,1)S(1)}, u32[]{:S(2)}, u32[]{:S(2)}) collective-permute-start(bf16[3,4352]{1,0:T(4,128)(2,1)S(1)} %slice.32), channel_id=1, source_target_pairs={{0,2},{2,4},{4,6},{6,8},{8,10},{10,12},{12,14},{14,16},{16,18},{18... | collective-permute-start | bytes 78344 | tf_op jit(solution)/shard_map/ppermute | solution.py:21
  8.3 2.1 %copy-start.3 = (f32[4352]{0:T(1024)S(1)}, f32[4352]{0:T(1024)}, u32[]{:S(2)}) copy-start(f32[4352]{0:T(1024)} %param.13) | copy-start | bytes 52228
  10.5 1.4 %copy-start = (bf16[128,4096]{1,0:T(8,128)(2,1)S(1)}, bf16[128,4096]{1,0:T(8,128)(2,1)}, u32[]{:S(2)}) copy-start(bf16[128,4096]{1,0:T(8,128)(2,1)} %gate.1) | copy-start | bytes 3145732
  10.5 1.4 %copy-start.1 = (f32[4096]{0:T(1024)S(1)}, f32[4096]{0:T(1024)}, u32[]{:S(2)}) copy-start(f32[4096]{0:T(1024)} %param.17) | copy-start | bytes 49156
